TPU v7x, 256 devices: a whole 4x4x8 slice. The times are simulated.
256 devices in a mesh: rep: 16 (over y_lo, z), slab: 16 (over y_hi, x, core).
Axes of the slice: x: 4, y: 4 (y_hi: 2, y_lo: 2; y = y_hi * 2 + y_lo), z: 8, core: 2. Of those that a mesh axis runs over, the one named last changes fastest.
Arguments:
- positions: float32 [16, 3, 98304], P('rep', None, 'slab'), as said below
- velocities: float32 [16, 3, 98304], P('rep', None, 'slab'), may hold values from -6 to 6
- strength: float32 [98304], P('slab'), may hold values from 0.5 to 2
- inv_mass: float32 [98304], P('slab'), may hold values from 0.25 to 1
- solute: int32 [98304], P('slab'), may hold values 0 or 1
- scales: float32 [16], P('rep'), may hold values from 0.3 to 1
- neighbours: int32 [768, 4], P('slab'), may hold values from 0 to 767, as said below
- counts: int32 [768], P('slab'), may hold values from 1 to 4
- partner: int32 [16], P('rep'), may hold values from 0 to 15, as said below
- accept: int32 [16], P('rep'), may hold values from 0 to 1, as said below
Outputs:
- new_positions: float32 [16, 3, 98304], P('rep', None, 'slab')
- new_velocities: float32 [16, 3, 98304], P('rep', None, 'slab')
- exponent: float32 [16], P('rep')
Inputs may be any that keep to these rules, and one draw needn't show every extreme that they name: `positions`: the x component of an atom of slab t (atoms t * 48 * 128 onward) lies in [t, t + 1); the others in [0, 2). `neighbours`: each listed block lies in the block's own slab, among the last 16 blocks of the previous slab, or among the first 16 blocks of the next slab, slabs taken periodically; every block lists itself first. Replicas are matched in pairs of neighbouring indices r and r + 1, all starting on the same parity; a replica left out is its own partner. `accept`: equal for both members of a pair; 0 for a replica that is its own partner.
All inputs are finite; a program needn't handle non-finite values. No bound on the sum of `solute` on one device may be relied on, other than what follows from the above.
Results may differ from a plain program's by a relative error of at most 0.0003.
Values sent between devices are 32-bit elements; how exact they have to be, the bound alone decides.
A program may use at most 64 MiB of HBM per device.

v0:
```python
import math

import jax
import jax.numpy as jnp
from jax import lax
from jax.sharding import PartitionSpec as P

NB = 4


SIGMA = 0.35
BOX = 2.0
STEP = 0.02
HIGH = lax.Precision.HIGHEST


def shifted(block, axis, distance):
    devices = range(lax.axis_size(axis))
    route = [(i - distance, i) for i in devices if i - distance in devices]
    return lax.ppermute(block, axis, route)


def padded(block, sides, width):
    for axis, dim in sides:
        count = lax.axis_size(axis)
        forward = [(i, i + 1) for i in range(count - 1)]
        forward.append((count - 1, 0))
        backward = [(target, source) for source, target in forward]
        low = lax.ppermute(
            lax.slice_in_dim(block, block.shape[dim] - width, None, axis=dim), axis, forward
        )
        high = lax.ppermute(lax.slice_in_dim(block, 0, width, axis=dim), axis, backward)
        block = jnp.concatenate([low, block, high], axis=dim)
    return block


def constants(periods):
    hcoef = jnp.array(
        [p * p / (2.0 * math.pi**2) / (2.0 * SIGMA**2) for p in periods], jnp.float32
    ).reshape(3, 1)
    shift = sum((p * p / (2.0 * math.pi**2) / (2.0 * SIGMA**2) for p in periods))
    fcoef = jnp.array([p / math.pi / (2.0 * SIGMA**2) for p in periods], jnp.float32).reshape(3, 1)
    factors = jnp.array([2.0 * math.pi / p for p in periods], jnp.float32).reshape(3, 1)
    return (hcoef, shift, fcoef, factors)


def angle_features(pos, factors):
    theta = pos * factors
    return (jnp.cos(theta), jnp.sin(theta))


def field_sums(ca_own, sa_own, ca_all, sa_all, cols_all, index, masks, hcoef, shift):
    own_c = (ca_own * hcoef).reshape(3, -1, 128)
    own_s = (sa_own * hcoef).reshape(3, -1, 128)
    blk_c = ca_all.reshape(3, -1, 128)
    blk_s = sa_all.reshape(3, -1, 128)
    blk_cols = cols_all.reshape(cols_all.shape[0], -1, 128)
    total = jnp.zeros((cols_all.shape[0],) + own_c.shape[1:], jnp.float32)
    for entry in range(len(masks)):
        pick = index[:, entry]
        far_c = jnp.take(blk_c, pick, axis=1)
        far_s = jnp.take(blk_s, pick, axis=1)
        far_cols = jnp.take(blk_cols, pick, axis=1)
        inner = jnp.einsum("cbi,cbj->bij", own_c, far_c, precision=HIGH) + jnp.einsum(
            "cbi,cbj->bij", own_s, far_s, precision=HIGH
        )
        kernel = jnp.exp(inner - shift)
        total = (
            total
            + jnp.einsum("bij,fbj->fbi", kernel, far_cols, precision=HIGH)
            * masks[entry][None, :, None]
        )
    return total.reshape(cols_all.shape[0], -1)


def take_shifted(state, below, above):
    lower_pos, lower_vel, lower_sum = shifted((state[0], state[1], state[2]), "rep", 1)
    upper_pos, upper_vel, upper_sum = shifted((state[0], state[1], state[2]), "rep", -1)
    pos, vel, summary = state
    other_pos = jnp.where(below, lower_pos, jnp.where(above, upper_pos, pos))
    other_vel = jnp.where(below, lower_vel, jnp.where(above, upper_vel, vel))
    other_sum = jnp.where(below, lower_sum, jnp.where(above, upper_sum, summary))
    return (other_pos, other_vel, other_sum)


def shards(
    positions, velocities, strength, inv_mass, solute, scales, neighbours, counts, partner, accept
):
    n_slab = lax.axis_size("slab")
    here = lax.axis_index("slab")
    atoms = positions.shape[2]
    blocks = atoms // 128
    width = blocks * 128
    periods = [float(n_slab), BOX, BOX]
    hcoef, shift, fcoef, factors = constants(periods)
    flags = solute.astype(jnp.float32)
    params = padded(jnp.stack([strength, flags]), (("slab", 1),), width)
    level = scales[0]
    root = jnp.sqrt(level)
    far_scale = params[0] * jnp.where(params[1] > 0.5, root, jnp.float32(1.0))
    own_scale = strength * jnp.where(flags > 0.5, root, jnp.float32(1.0))
    owner = neighbours // blocks
    local = neighbours % blocks
    gap = (owner - here) % n_slab
    index = jnp.where(
        gap == 0,
        blocks + local,
        jnp.where(gap == 1, blocks + blocks + local, local - (blocks - blocks)),
    )
    masks = [(counts > entry).astype(jnp.float32) for entry in range(NB)]

    def spread(pos):
        wide = padded(pos, (("slab", 1),), width)
        ca_all, sa_all = angle_features(wide, factors)
        ca_own = ca_all[:, width : width + atoms]
        sa_own = sa_all[:, width : width + atoms]
        return (ca_all, sa_all, ca_own, sa_own)

    pos = positions[0]
    vel = velocities[0]
    for turn in range(2):
        force_ca_all, force_sa_all, force_ca_own, force_sa_own = spread(pos)
        force_cols = jnp.concatenate([far_scale * force_ca_all, far_scale * force_sa_all], axis=0)
        force_sums = field_sums(
            force_ca_own,
            force_sa_own,
            force_ca_all,
            force_sa_all,
            force_cols,
            index,
            masks,
            hcoef,
            shift,
        )
        vel = vel + STEP * inv_mass * (
            fcoef * own_scale * (force_sa_own * force_sums[:3] - force_ca_own * force_sums[3:])
        )
        pos = pos + STEP * vel
    ca_all, sa_all, ca_own, sa_own = spread(pos)
    cols = jnp.stack([params[0] * params[1], params[0]])
    sums = field_sums(ca_own, sa_own, ca_all, sa_all, cols, index, masks, hcoef, shift)
    inside, every = (sums[0], sums[1])
    solute_part = 0.5 * jnp.sum(strength * flags * inside)
    mixed_part = 0.5 * jnp.sum(strength * (flags * (every - inside) + (1.0 - flags) * inside))
    solute_sum, mixed_sum = lax.psum((solute_part, mixed_part), "slab")
    summary = jnp.stack([solute_sum, mixed_sum, level])
    mine = lax.axis_index("rep")
    mate = partner[0]
    below = mate == mine - 1
    above = mate == mine + 1
    state = (pos, vel, summary)
    other_pos, other_vel, other_sum = take_shifted(state, below, above)
    total_atoms = atoms * n_slab
    exponent = (
        (other_sum[2] - level) * (solute_sum - other_sum[0])
        + (jnp.sqrt(other_sum[2]) - root) * (mixed_sum - other_sum[1])
    ) / total_atoms
    taken = accept[0] == 1
    new_pos = jnp.where(taken, other_pos, pos)
    new_vel = jnp.where(taken, other_vel, vel)
    return (new_pos[None], new_vel[None], exponent.reshape(1))


def solution(mesh):
    placed = (
        P("rep", None, "slab"),
        P("rep", None, "slab"),
        P("slab"),
        P("slab"),
        P("slab"),
        P("rep"),
        P("slab", None),
        P("slab"),
        P("rep"),
        P("rep"),
    )
    return jax.shard_map(
        shards,
        mesh=mesh,
        in_specs=placed,
        out_specs=(P("rep", None, "slab"), P("rep", None, "slab"), P("rep")),
        check_vma=False,
    )
```

profile of v0, /device:TPU:8, one launch (start us, length us, event | category | flops | bytes accessed | tf_op | source)
XLA Modules:
  0.0 337.4 jit_solution(14883816392632288701)
XLA Ops:
  37.2 5.6 %fusion.206 = f32[48,128,128]{2,1,0:T(8,128)S(1)} fusion(f32[48,3,128]{2,1,0:T(4,128)S(1)} %gather_fusion.11, pred[48]{0:T(512)(128)(4,1)S(1)} %get-tuple-element.41, f32[3,18432]{1,0:T(4,128)S(1)} %maximum_multiply_fusion, f32[3]{0:T(128)S(1)} %copy-done.2), kind=kOutput, calls=%fused_computation.216 | convolution fusion | flops 28348416 | bytes 3343360 | tf_op jit(solution)/shard_map/cbi,cbj->bij/dot_general | solution.py:64
  48.3 5.4 %fusion.210 = f32[48,128,128]{2,1,0:T(8,128)S(1)} fusion(f32[48,3,128]{2,1,0:T(4,128)S(1)} %gather_fusion.8, pred[48]{0:T(512)(128)(4,1)S(1)} %get-tuple-element.43, f32[3,18432]{1,0:T(4,128)S(1)} %maximum_multiply_fusion, f32[3]{0:T(128)S(1)} %copy-done.2), kind=kOutput, calls=%fused_computation.220 | convolution fusion | flops 28348416 | bytes 3343360 | tf_op jit(solution)/shard_map/cbi,cbj->bij/dot_general | solution.py:64
  53.8 5.7 %fusion.216 = f32[48,128,128]{2,1,0:T(8,128)S(1)} fusion(f32[48,3,128]{2,1,0:T(4,128)S(1)} %gather_fusion.4, pred[48]{0:T(512)(128)(4,1)S(1)} %get-tuple-element.45, f32[3,18432]{1,0:T(4,128)S(1)} %maximum_multiply_fusion, f32[3]{0:T(128)S(1)} %copy-done.2), kind=kOutput, calls=%fused_computation.226 | convolution fusion | flops 28348416 | bytes 3343360 | tf_op jit(solution)/shard_map/cbi,cbj->bij/dot_general | solution.py:64
  59.4 5.5 %fusion.214 = f32[48,128,128]{2,1,0:T(8,128)S(1)} fusion(f32[48,3,128]{2,1,0:T(4,128)S(1)} %gather_fusion.5, pred[48]{0:T(512)(128)(4,1)S(1)} %get-tuple-element.45, f32[3,18432]{1,0:T(4,128)S(1)} %maximum_multiply_fusion, f32[3]{0:T(128)S(1)} %copy-done.2), kind=kOutput, calls=%fused_computation.224 | convolution fusion | flops 28348416 | bytes 3343360 | tf_op jit(solution)/shard_map/cbi,cbj->bij/dot_general | solution.py:64
  64.9 5.8 %fusion.224 = f32[48,128,128]{2,1,0:T(8,128)S(1)} fusion(f32[48,3,128]{2,1,0:T(4,128)S(1)} %gather_fusion.1, pred[48]{0:T(512)(128)(4,1)S(1)} %get-tuple-element.18, f32[3,18432]{1,0:T(4,128)S(1)} %maximum_multiply_fusion, f32[3]{0:T(128)S(1)} %copy-done.2), kind=kOutput, calls=%fused_computation.234 | convolution fusion | flops 28348416 | bytes 3343360 | tf_op jit(solution)/shard_map/cbi,cbj->bij/dot_general | solution.py:64
  70.7 5.5 %fusion.218 = f32[48,128,128]{2,1,0:T(8,128)S(1)} fusion(f32[48,3,128]{2,1,0:T(4,128)S(1)} %gather_fusion.2, pred[48]{0:T(512)(128)(4,1)S(1)} %get-tuple-element.18, f32[3,18432]{1,0:T(4,128)S(1)} %maximum_multiply_fusion, f32[3]{0:T(128)S(1)} %copy-done.2), kind=kOutput, calls=%fused_computation.228 | convolution fusion | flops 28348416 | bytes 3343360 | tf_op jit(solution)/shard_map/cbi,cbj->bij/dot_general | solution.py:64
  91.7 5.5 %fusion.72 = f32[6,48,128]{2,0,1:T(8,128)S(1)} fusion(f32[48,6,128]{2,1,0:T(8,128)S(1)} %fusion.81, f32[48,6,128]{2,1,0:T(8,128)S(1)} %fusion.78, f32[48,6,128]{2,1,0:T(8,128)S(1)} %fusion.75, f32[48,128,128]{2,1,0:T(8,128)S(1)} %fusion.224, f32[48,128,128]{2,1,0:T(8,128)S(1)} %fusion.218, f32[48,6,128]{2,1,0:T(8,128)S(1)} %gather_fusion, ...), kind=kOutput, calls=%fused_computation.100 | convolution fusion | flops 58380288 | bytes 7028976 | tf_op jit(solution)/shard_map/bij,fbj->fbi/dot_general | solution.py:70
  124.9 5.6 %fusion.182 = f32[48,128,128]{2,1,0:T(8,128)S(1)} fusion(f32[48,3,128]{2,1,0:T(4,128)S(1)} %gather_fusion.23, pred[48]{0:T(512)(128)(4,1)S(1)} %get-tuple-element.41, f32[3,18432]{1,0:T(4,128)S(1)} %maximum_multiply_fusion.2, f32[3]{0:T(128)S(1)} %copy-done.2), kind=kOutput, calls=%fused_computation.192 | convolution fusion | flops 28348416 | bytes 3343360 | tf_op jit(solution)/shard_map/cbi,cbj->bij/dot_general | solution.py:64
  136.0 5.5 %fusion.186 = f32[48,128,128]{2,1,0:T(8,128)S(1)} fusion(f32[48,3,128]{2,1,0:T(4,128)S(1)} %gather_fusion.20, pred[48]{0:T(512)(128)(4,1)S(1)} %get-tuple-element.43, f32[3,18432]{1,0:T(4,128)S(1)} %maximum_multiply_fusion.2, f32[3]{0:T(128)S(1)} %copy-done.2), kind=kOutput, calls=%fused_computation.196 | convolution fusion | flops 28348416 | bytes 3343360 | tf_op jit(solution)/shard_map/cbi,cbj->bij/dot_general | solution.py:64
  141.5 5.6 %fusion.192 = f32[48,128,128]{2,1,0:T(8,128)S(1)} fusion(f32[48,3,128]{2,1,0:T(4,128)S(1)} %gather_fusion.16, pred[48]{0:T(512)(128)(4,1)S(1)} %get-tuple-element.45, f32[3,18432]{1,0:T(4,128)S(1)} %maximum_multiply_fusion.2, f32[3]{0:T(128)S(1)} %copy-done.2), kind=kOutput, calls=%fused_computation.202 | convolution fusion | flops 28348416 | bytes 3343360 | tf_op jit(solution)/shard_map/cbi,cbj->bij/dot_general | solution.py:64
  147.1 5.5 %fusion.190 = f32[48,128,128]{2,1,0:T(8,128)S(1)} fusion(f32[48,3,128]{2,1,0:T(4,128)S(1)} %gather_fusion.17, pred[48]{0:T(512)(128)(4,1)S(1)} %get-tuple-element.45, f32[3,18432]{1,0:T(4,128)S(1)} %maximum_multiply_fusion.2, f32[3]{0:T(128)S(1)} %copy-done.2), kind=kOutput, calls=%fused_computation.200 | convolution fusion | flops 28348416 | bytes 3343360 | tf_op jit(solution)/shard_map/cbi,cbj->bij/dot_general | solution.py:64
  152.6 5.8 %fusion.200 = f32[48,128,128]{2,1,0:T(8,128)S(1)} fusion(f32[48,3,128]{2,1,0:T(4,128)S(1)} %gather_fusion.13, pred[48]{0:T(512)(128)(4,1)S(1)} %get-tuple-element.18, f32[3,18432]{1,0:T(4,128)S(1)} %maximum_multiply_fusion.2, f32[3]{0:T(128)S(1)} %copy-done.2), kind=kOutput, calls=%fused_computation.210 | convolution fusion | flops 28348416 | bytes 3343360 | tf_op jit(solution)/shard_map/cbi,cbj->bij/dot_general | solution.py:64
  158.4 5.5 %fusion.194 = f32[48,128,128]{2,1,0:T(8,128)S(1)} fusion(f32[48,3,128]{2,1,0:T(4,128)S(1)} %gather_fusion.14, pred[48]{0:T(512)(128)(4,1)S(1)} %get-tuple-element.18, f32[3,18432]{1,0:T(4,128)S(1)} %maximum_multiply_fusion.2, f32[3]{0:T(128)S(1)} %copy-done.2), kind=kOutput, calls=%fused_computation.204 | convolution fusion | flops 28348416 | bytes 3343360 | tf_op jit(solution)/shard_map/cbi,cbj->bij/dot_general | solution.py:64
  179.4 5.5 %fusion.96 = f32[6,48,128]{2,0,1:T(8,128)S(1)} fusion(f32[48,6,128]{2,1,0:T(8,128)S(1)} %fusion.105, f32[48,6,128]{2,1,0:T(8,128)S(1)} %fusion.102, f32[48,6,128]{2,1,0:T(8,128)S(1)} %fusion.99, f32[48,128,128]{2,1,0:T(8,128)S(1)} %fusion.200, f32[48,128,128]{2,1,0:T(8,128)S(1)} %fusion.194, f32[48,6,128]{2,1,0:T(8,128)S(1)} %gather_fusion.12, ...), kind=kOutput, calls=%fused_computation.108 | convolution fusion | flops 58380288 | bytes 7028976 | tf_op jit(solution)/shard_map/bij,fbj->fbi/dot_general | solution.py:70
  192.7 6.6 %collective-permute-start.7 = (f32[3,6144]{1,0:T(4,128)S(1)}, f32[3,6144]{1,0:T(4,128)S(1)}, u32[]{:S(2)}, u32[]{:S(2)}) collective-permute-start(f32[3,6144]{1,0:T(4,128)S(1)} %get-tuple-element.10), channel_id=1, source_target_pairs={{16,0},{32,16},{48,32},{64,48},{80,64},{96,80},{112,96},{128,112},... | collective-permute-start | bytes 221192 | tf_op jit(solution)/shard_map/ppermute | solution.py:20
  214.6 5.6 %fusion.166 = f32[48,128,128]{2,1,0:T(8,128)S(1)} fusion(f32[48,3,128]{2,1,0:T(4,128)S(1)} %gather_fusion.29, pred[48]{0:T(512)(128)(4,1)S(1)} %get-tuple-element.45, f32[3,18432]{1,0:T(4,128)S(1)} %maximum_multiply_fusion.4, f32[3]{0:T(128)S(1)} %copy-done.2), kind=kOutput, calls=%fused_computation.176 | convolution fusion | flops 28348416 | bytes 3343360 | tf_op jit(solution)/shard_map/cbi,cbj->bij/dot_general | solution.py:64
  225.7 5.4 %fusion.170 = f32[48,128,128]{2,1,0:T(8,128)S(1)} fusion(f32[48,3,128]{2,1,0:T(4,128)S(1)} %gather_fusion.26, pred[48]{0:T(512)(128)(4,1)S(1)} %get-tuple-element.18, f32[3,18432]{1,0:T(4,128)S(1)} %maximum_multiply_fusion.4, f32[3]{0:T(128)S(1)} %copy-done.2), kind=kOutput, calls=%fused_computation.180 | convolution fusion | flops 28348416 | bytes 3343360 | tf_op jit(solution)/shard_map/cbi,cbj->bij/dot_general | solution.py:64
  231.1 5.7 %fusion.164 = f32[48,128,128]{2,1,0:T(8,128)S(1)} fusion(f32[48,3,128]{2,1,0:T(4,128)S(1)} %gather_fusion.31, pred[48]{0:T(512)(128)(4,1)S(1)} %get-tuple-element.43, f32[3,18432]{1,0:T(4,128)S(1)} %maximum_multiply_fusion.4, f32[3]{0:T(128)S(1)} %copy-done.2), kind=kOutput, calls=%fused_computation.174 | convolution fusion | flops 28348416 | bytes 3343360 | tf_op jit(solution)/shard_map/cbi,cbj->bij/dot_general | solution.py:64
  236.8 5.5 %fusion.162 = f32[48,128,128]{2,1,0:T(8,128)S(1)} fusion(f32[48,3,128]{2,1,0:T(4,128)S(1)} %gather_fusion.32, pred[48]{0:T(512)(128)(4,1)S(1)} %get-tuple-element.43, f32[3,18432]{1,0:T(4,128)S(1)} %maximum_multiply_fusion.4, f32[3]{0:T(128)S(1)} %copy-done.2), kind=kOutput, calls=%fused_computation.172 | convolution fusion | flops 28348416 | bytes 3343360 | tf_op jit(solution)/shard_map/cbi,cbj->bij/dot_general | solution.py:64
  242.3 5.9 %fusion.160 = f32[48,128,128]{2,1,0:T(8,128)S(1)} fusion(f32[48,3,128]{2,1,0:T(4,128)S(1)} %gather_fusion.34, pred[48]{0:T(512)(128)(4,1)S(1)} %get-tuple-element.41, f32[3,18432]{1,0:T(4,128)S(1)} %maximum_multiply_fusion.4, f32[3]{0:T(128)S(1)} %copy-done.2), kind=kOutput, calls=%fused_computation.170 | convolution fusion | flops 28348416 | bytes 3343360 | tf_op jit(solution)/shard_map/cbi,cbj->bij/dot_general | solution.py:64
  248.2 5.5 %fusion.158 = f32[48,128,128]{2,1,0:T(8,128)S(1)} fusion(f32[48,3,128]{2,1,0:T(4,128)S(1)} %gather_fusion.35, pred[48]{0:T(512)(128)(4,1)S(1)} %get-tuple-element.41, f32[3,18432]{1,0:T(4,128)S(1)} %maximum_multiply_fusion.4, f32[3]{0:T(128)S(1)} %copy-done.2), kind=kOutput, calls=%fused_computation.168 | convolution fusion | flops 28348416 | bytes 3343360 | tf_op jit(solution)/shard_map/cbi,cbj->bij/dot_general | solution.py:64
  276.1 6.0 %collective-permute-start.9 = (f32[3,6144]{1,0:T(4,128)S(1)}, f32[3,6144]{1,0:T(4,128)S(1)}, u32[]{:S(2)}, u32[]{:S(2)}) collective-permute-start(f32[3,6144]{1,0:T(4,128)S(1)} %get-tuple-element.11), channel_id=1, source_target_pairs={{16,0},{32,16},{48,32},{64,48},{80,64},{96,80},{112,96},{128,112},... | collective-permute-start | bytes 221192 | tf_op jit(solution)/shard_map/ppermute | solution.py:20
  282.2 37.2 %all-reduce = (f32[]{:T(128)}, f32[]{:T(128)}) all-reduce(f32[]{:T(128)S(6)} %mul.373, f32[]{:T(128)S(6)} %mul.369), channel_id=1, replica_groups=mesh['rep'=16,'slab'=16] {'slab'}, use_global_device_ids=true, to_apply=%region_3.7 | all-reduce | flops 2 | bytes 16 | tf_op jit(solution)/shard_map/psum | solution.py:145
  322.6 6.0 %collective-permute-start.13 = (f32[3]{0:T(128)S(1)}, f32[3]{0:T(128)S(1)}, u32[]{:S(2)}, u32[]{:S(2)}) collective-permute-start(f32[3]{0:T(128)S(1)} %pad_maximum_fusion.5), channel_id=1, source_target_pairs={{16,0},{32,16},{48,32},{64,48},{80,64},{96,80},{112,96},{128,112},... | collective-permute-start | bytes 44 | tf_op jit(solution)/shard_map/ppermute | solution.py:20
  (124 shorter events, 160.4 us)
Async XLA Ops:
  2.2 29.5 %copy-start.5 = (f32[3]{0:T(128)S(1)}, f32[3]{0:T(128)}, u32[]{:S(2)}) copy-start(f32[3]{0:T(128)} %constant.120.clone) | copy-start | bytes 40
  2.2 14.9 %collective-permute-start.3 = (f32[2,6144]{1,0:T(2,128)S(1)}, f32[2,6144]{1,0:T(2,128)S(1)}, u32[]{:S(2)}, u32[]{:S(2)}) collective-permute-start(f32[2,6144]{1,0:T(2,128)S(1)} %pad_maximum_fusion.4), channel_id=1, source_target_pairs={{1,0},{2,1},{3,2},{4,3},{5,4},{6,5},{7,6},{8,7},{9,8},{10,9},{11,1... | collective-permute-start | bytes 147464 | tf_op jit(solution)/shard_map/ppermute | solution.py:32
  6.2 10.9 %collective-permute-start.2 = (f32[2,6144]{1,0:T(2,128)S(1)}, f32[2,6144]{1,0:T(2,128)S(1)}, u32[]{:S(2)}, u32[]{:S(2)}) collective-permute-start(f32[2,6144]{1,0:T(2,128)S(1)} %pad_maximum_fusion.4), channel_id=1, source_target_pairs={{0,1},{1,2},{2,3},{3,4},{4,5},{5,6},{6,7},{7,8},{8,9},{9,10},{10,1... | collective-permute-start | bytes 147464 | tf_op jit(solution)/shard_map/ppermute | solution.py:29
  7.1 11.0 %collective-permute-start.1 = (f32[3,6144]{1,0:T(4,128)S(1)}, f32[3,6144]{1,0:T(4,128)S(1)}, u32[]{:S(2)}, u32[]{:S(2)}) collective-permute-start(f32[3,6144]{1,0:T(4,128)S(1)} %bitcast.281), channel_id=1, source_target_pairs={{1,0},{2,1},{3,2},{4,3},{5,4},{6,5},{7,6},{8,7},{9,8},{10,9},{11,1... | collective-permute-start | bytes 221192 | tf_op jit(solution)/shard_map/ppermute | solution.py:32
  12.5 7.7 %collective-permute-start = (f32[3,6144]{1,0:T(4,128)S(1)}, f32[3,6144]{1,0:T(4,128)S(1)}, u32[]{:S(2)}, u32[]{:S(2)}) collective-permute-start(f32[3,6144]{1,0:T(4,128)S(1)} %bitcast.282), channel_id=1, source_target_pairs={{0,1},{1,2},{2,3},{3,4},{4,5},{5,6},{6,7},{7,8},{8,9},{9,10},{10,1... | collective-permute-start | bytes 221192 | tf_op jit(solution)/shard_map/ppermute | solution.py:29
  17.1 14.7 %copy-start.2 = (f32[3]{0:T(128)S(1)}, f32[3]{0:T(128)}, u32[]{:S(2)}) copy-start(f32[3]{0:T(128)} %constant.118.clone) | copy-start | bytes 40
  91.7 5.5 %copy-start = (f32[1,3,6144]{2,0,1:T(1,128)S(1)}, f32[1,3,6144]{2,0,1:T(1,128)}, u32[]{:S(2)}) copy-start(f32[1,3,6144]{2,0,1:T(1,128)} %param.19) | copy-start | bytes 221188
  91.7 5.5 %copy-start.4 = (f32[1,3,6144]{2,0,1:T(1,128)S(1)}, f32[1,3,6144]{2,0,1:T(1,128)}, u32[]{:S(2)}) copy-start(f32[1,3,6144]{2,0,1:T(1,128)} %param.20) | copy-start | bytes 221188
  91.7 5.5 %copy-start.6 = (f32[3]{0:T(128)S(1)}, f32[3]{0:T(128)}, u32[]{:S(2)}) copy-start(f32[3]{0:T(128)} %constant.119.clone) | copy-start | bytes 40
  98.0 5.6 %collective-permute-start.5 = (f32[3,6144]{1,0:T(4,128)S(1)}, f32[3,6144]{1,0:T(4,128)S(1)}, u32[]{:S(2)}, u32[]{:S(2)}) collective-permute-start(f32[3,6144]{1,0:T(4,128)S(1)} %get-tuple-element.16), channel_id=1, source_target_pairs={{1,0},{2,1},{3,2},{4,3},{5,4},{6,5},{7,6},{8,7},{9,8},{10,9},{11,1... | collective-permute-start | bytes 221192 | tf_op jit(solution)/shard_map/ppermute | solution.py:32
  101.4 7.7 %collective-permute-start.4 = (f32[3,6144]{1,0:T(4,128)S(1)}, f32[3,6144]{1,0:T(4,128)S(1)}, u32[]{:S(2)}, u32[]{:S(2)}) collective-permute-start(f32[3,6144]{1,0:T(4,128)S(1)} %get-tuple-element.16), channel_id=1, source_target_pairs={{0,1},{1,2},{2,3},{3,4},{4,5},{5,6},{6,7},{7,8},{8,9},{9,10},{10,1... | collective-permute-start | bytes 221192 | tf_op jit(solution)/shard_map/ppermute | solution.py:29
  185.7 15.7 %collective-permute-start.11 = (f32[3,6144]{1,0:T(4,128)S(1)}, f32[3,6144]{1,0:T(4,128)S(1)}, u32[]{:S(2)}, u32[]{:S(2)}) collective-permute-start(f32[3,6144]{1,0:T(4,128)S(1)} %get-tuple-element.10), channel_id=1, source_target_pairs={{1,0},{2,1},{3,2},{4,3},{5,4},{6,5},{7,6},{8,7},{9,8},{10,9},{11,1... | collective-permute-start | bytes 221192 | tf_op jit(solution)/shard_map/ppermute | solution.py:32
  185.7 15.6 %collective-permute-start.10 = (f32[3,6144]{1,0:T(4,128)S(1)}, f32[3,6144]{1,0:T(4,128)S(1)}, u32[]{:S(2)}, u32[]{:S(2)}) collective-permute-start(f32[3,6144]{1,0:T(4,128)S(1)} %get-tuple-element.10), channel_id=1, source_target_pairs={{0,1},{1,2},{2,3},{3,4},{4,5},{5,6},{6,7},{7,8},{8,9},{9,10},{10,1... | collective-permute-start | bytes 221192 | tf_op jit(solution)/shard_map/ppermute | solution.py:29
  188.9 133.7 %collective-permute-start.6 = (f32[3,6144]{1,0:T(4,128)S(1)}, f32[3,6144]{1,0:T(4,128)S(1)}, u32[]{:S(2)}, u32[]{:S(2)}) collective-permute-start(f32[3,6144]{1,0:T(4,128)S(1)} %get-tuple-element.10), channel_id=1, source_target_pairs={{0,16},{16,32},{32,48},{48,64},{64,80},{80,96},{96,112},{112,128},... | collective-permute-start | bytes 221192 | tf_op jit(solution)/shard_map/ppermute | solution.py:20
  192.7 135.9 %collective-permute-start.7 = (f32[3,6144]{1,0:T(4,128)S(1)}, f32[3,6144]{1,0:T(4,128)S(1)}, u32[]{:S(2)}, u32[]{:S(2)}) collective-permute-start(f32[3,6144]{1,0:T(4,128)S(1)} %get-tuple-element.10), channel_id=1, source_target_pairs={{16,0},{32,16},{48,32},{64,48},{80,64},{96,80},{112,96},{128,112},... | collective-permute-start | bytes 221192 | tf_op jit(solution)/shard_map/ppermute | solution.py:20
  199.4 130.0 %collective-permute-start.8 = (f32[3,6144]{1,0:T(4,128)S(1)}, f32[3,6144]{1,0:T(4,128)S(1)}, u32[]{:S(2)}, u32[]{:S(2)}) collective-permute-start(f32[3,6144]{1,0:T(4,128)S(1)} %get-tuple-element.11), channel_id=1, source_target_pairs={{0,16},{16,32},{32,48},{48,64},{64,80},{80,96},{96,112},{112,128},... | collective-permute-start | bytes 221192 | tf_op jit(solution)/shard_map/ppermute | solution.py:20
  269.1 5.2 %copy-start.1 = (f32[6144]{0:T(1024)S(1)}, f32[6144]{0:T(1024)}, u32[]{:S(2)}) copy-start(f32[6144]{0:T(1024)} %param.21) | copy-start | bytes 73732
  269.1 5.2 %copy-start.3 = (s32[6144]{0:T(1024)S(1)}, s32[6144]{0:T(1024)}, u32[]{:S(2)}) copy-start(s32[6144]{0:T(1024)} %param.23) | copy-start | bytes 73732
  276.1 53.3 %collective-permute-start.9 = (f32[3,6144]{1,0:T(4,128)S(1)}, f32[3,6144]{1,0:T(4,128)S(1)}, u32[]{:S(2)}, u32[]{:S(2)}) collective-permute-start(f32[3,6144]{1,0:T(4,128)S(1)} %get-tuple-element.11), channel_id=1, source_target_pairs={{16,0},{32,16},{48,32},{64,48},{80,64},{96,80},{112,96},{128,112},... | collective-permute-start | bytes 221192 | tf_op jit(solution)/shard_map/ppermute | solution.py:20
  320.7 9.4 %collective-permute-start.12 = (f32[3]{0:T(128)S(1)}, f32[3]{0:T(128)S(1)}, u32[]{:S(2)}, u32[]{:S(2)}) collective-permute-start(f32[3]{0:T(128)S(1)} %pad_maximum_fusion.5), channel_id=1, source_target_pairs={{0,16},{16,32},{32,48},{48,64},{64,80},{80,96},{96,112},{112,128},... | collective-permute-start | bytes 44 | tf_op jit(solution)/shard_map/ppermute | solution.py:20
  322.6 7.5 %collective-permute-start.13 = (f32[3]{0:T(128)S(1)}, f32[3]{0:T(128)S(1)}, u32[]{:S(2)}, u32[]{:S(2)}) collective-permute-start(f32[3]{0:T(128)S(1)} %pad_maximum_fusion.5), channel_id=1, source_target_pairs={{16,0},{32,16},{48,32},{64,48},{80,64},{96,80},{112,96},{128,112},... | collective-permute-start | bytes 44 | tf_op jit(solution)/shard_map/ppermute | solution.py:20
where the time goes:
time: 342 us; the launch traced here: 337 us
  matrix products  196 us (57%)
  starting transfers between devices  39.8 us (12%)
  blocking collectives  37.2 us (11%)
  local copies, waits for them, and re-layouts  26.5 us (8%)
  other arithmetic  20.1 us (6%)
  between operations  9.63 us (3%)
  waiting for transfers between devices  8.43 us (2%)
    dot_general x12, matrix products, field_sums(): jnp.einsum('cbi,cbj->bij', own_c, far_c, precision=HIGH)  67.2 us
    dot_general x12, matrix products, field_sums(): jnp.einsum('cbi,cbj->bij', own_s, far_s, precision=HIGH)  65.9 us
    dot_general x12, matrix products, field_sums(): jnp.einsum('bij,fbj->fbi', kernel, far_cols, precision=HIGH)  62.5 us
    psum x1, blocking collectives, shards(): solute_sum, mixed_sum = lax.psum((solute_part, mixed_part), 'slab')  37.2 us
    ppermute x6, starting transfers between devices, shifted(): return lax.ppermute(block, axis, route)  26.4 us
    ppermute x4, starting transfers between devices, padded(): lax.ppermute(lax.slice_in_dim(block, 0, width, axis=dim), axis, backward)  13 us
    gather x12, local copies, waits for them, and re-layouts, field_sums(): far_c = jnp.take(blk_c, pick, axis=1)  7.57 us
    gather x12, local copies, waits for them, and re-layouts, field_sums(): far_s = jnp.take(blk_s, pick, axis=1)  7.57 us
  transfers between devices with their start and end apart: 14, of which 3 were waited for; matrix products, arithmetic and copies ran while one was open for 25% of the time, Pallas kernels for 0%

commit v1 on v0

v1 whole, which is shorter than its diff:
```python
import functools
import math

import jax
import jax.numpy as jnp
from jax import lax
from jax.experimental import pallas as pl
from jax.experimental.pallas import tpu as pltpu
from jax.sharding import PartitionSpec as P

NB = 4
RIM = 16
SIGMA = 0.35
BOX = 2.0
STEP = 0.02
NONE = -1000.0
MESH = pl.DeviceIdType.MESH
F32 = jnp.float32
BF16 = jnp.bfloat16
SINE = (
    6.28318530717,
    -41.34170211,
    81.60522621,
    -76.70428132,
    42.00980576,
    -14.39413556,
)


def dot(a, b):
    return jnp.dot(a, b, preferred_element_type=F32)


def dot_left(a, b):
    return lax.dot_general(a, b, (((0,), (0,)), ((), ())), preferred_element_type=F32)


def parts(value):
    first = value.astype(BF16).astype(F32)
    rest = value - first
    second = rest.astype(BF16).astype(F32)
    third = rest - second
    return first, second, third


def kernel(
    n_rep,
    n_slab,
    blocks,
    scales,
    listed,
    counts,
    partner,
    accept,
    positions,
    velocities,
    strength,
    inv_mass,
    solute,
    new_pos,
    new_vel,
    exponent,
    pick,
    pos8,
    vel8,
    feat8,
    own,
    far,
    flagged,
    acc,
    rows,
    stage,
    halo,
    state,
    swapped,
    energy,
    summary,
    halo_send,
    halo_recv,
    state_send,
    state_recv,
    energy_send,
    energy_recv,
    summary_send,
    summary_recv,
):
    rep = lax.axis_index("rep")
    here = lax.axis_index("slab")
    above = {"rep": lax.rem(rep + 1, n_rep)}
    below = {"rep": lax.rem(rep + n_rep - 1, n_rep)}
    after = {"slab": lax.rem(here + 1, n_slab)}
    before = {"slab": lax.rem(here + n_slab - 1, n_slab)}
    wide = blocks + 2 * RIM

    barrier = pltpu.get_barrier_semaphore()
    for other in range(1, n_slab):
        pl.semaphore_signal(
            barrier, 1, device_id={"slab": lax.rem(here + other, n_slab)}, device_id_type=MESH
        )
    for other in (below, above):
        pl.semaphore_signal(barrier, 1, device_id=other, device_id_type=MESH)

    row = lax.broadcasted_iota(jnp.int32, (8, 128), 0)
    long = (row == 0) | (row == 4)
    is3 = row == 3
    is7 = row == 7
    periods = (float(n_slab), BOX)
    inverse = jnp.where(long, F32(1.0 / periods[0]), F32(1.0 / periods[1]))
    phase = jnp.where(row >= 4, F32(0.25), F32(0.0))
    heights = [p * p / (2.0 * math.pi**2) / (2.0 * SIGMA**2) for p in periods]
    height = jnp.where(long, F32(heights[0]), F32(heights[1]))
    shift = heights[0] + 2.0 * heights[1]
    slope = jnp.where(
        long,
        F32(STEP * periods[0] / math.pi / (2.0 * SIGMA**2)),
        F32(STEP * periods[1] / math.pi / (2.0 * SIGMA**2)),
    )
    slope = jnp.where(is3 | is7, F32(0.0), jnp.where(row >= 4, -slope, slope))

    def features(x):
        turn = x * inverse - phase
        turn = turn - jnp.floor(turn + 0.5)
        w = 0.25 - jnp.abs(turn)
        z = w * w
        value = F32(SINE[-1])
        for c in SINE[-2::-1]:
            value = value * z + F32(c)
        return value * w

    def put_far(spot, value, log_weight):
        value = jnp.where(is3, F32(1.0), jnp.where(is7, log_weight, value))
        a, b, c = parts(value)
        far[spot] = jnp.concatenate([a, b, c, a, b, a], axis=0).astype(BF16)

    def put_own(b, value):
        value = jnp.where(is3, F32(-shift), jnp.where(is7, F32(1.0), value * height))
        x, y, z = parts(value)
        own[b] = jnp.concatenate([x, x, x, y, y, z], axis=0).astype(BF16)

    level = jnp.full((8, 128), scales[0], F32)
    root = jnp.sqrt(level)

    def atom_rows(t, carry):
        at = pl.ds(pl.multiple_of(t * 8, 8), 8)
        plain = strength[at, :]
        chosen = solute[at, :] == 1
        scaled = plain * jnp.where(chosen, root, F32(1.0))
        rows[0, at, :] = jnp.log(scaled)
        rows[1, at, :] = jnp.log(plain)
        rows[2, at, :] = jnp.where(chosen, F32(1.0), F32(0.0))
        rows[3, at, :] = scaled * inv_mass[at, :]
        return carry

    lax.fori_loop(0, blocks // 8, atom_rows, 0)

    def one_row(which, b):
        return rows[which, pl.ds(b, 1), :]

    def put_stage(turn, side, i, x, extra):
        stage[turn, side, i] = jnp.where(is3, extra, x)[:4]

    def load(b):
        blank = jnp.zeros((1, 128), F32)
        x = positions[pl.ds(b, 3, stride=blocks), :]
        v = velocities[pl.ds(b, 3, stride=blocks), :]
        pos8[b] = jnp.concatenate([x, blank, x, blank], axis=0)
        vel8[b] = jnp.concatenate([v, blank, v, blank], axis=0)

    def load_some(t, carry):
        for u in range(4):
            load(t * 4 + u)
        return carry

    lax.fori_loop(0, blocks // 4, load_some, 0)

    def stage_first(i, carry):
        low = i
        high = blocks - RIM + i
        put_stage(0, 0, i, pos8[low], one_row(0, low))
        put_stage(0, 1, i, pos8[high], one_row(0, high))
        return carry

    lax.fori_loop(0, RIM, stage_first, 0)
    pl.semaphore_wait(barrier, n_slab - 1 + 2)

    def halo_copy(turn, side):
        return pltpu.make_async_remote_copy(
            src_ref=stage.at[turn, side],
            dst_ref=halo.at[turn, side],
            send_sem=halo_send.at[turn, side],
            recv_sem=halo_recv.at[turn, side],
            device_id=before if side == 0 else after,
            device_id_type=MESH,
        )

    def send_halo(turn):
        for side in range(2):
            halo_copy(turn, side).start()

    send_halo(0)

    first = here * blocks
    total = n_slab * blocks

    def find(b, carry):
        count = counts[b]
        for k in range(1, NB):
            near = listed[k, b] - first
            near = jnp.where(near < 0, near + total, near)
            near = jnp.where(near < blocks + RIM, near, near - (total - blocks - 2 * RIM))
            pick[b * NB + k] = jnp.where(k < count, near, wide)
        return carry

    lax.fori_loop(0, blocks, find, 0)

    far[wide] = jnp.concatenate(
        [jnp.where(is7, F32(NONE), F32(0.0)), jnp.zeros((40, 128), F32)], axis=0
    ).astype(BF16)

    def own_features(which):
        def some(t, carry):
            for u in range(4):
                b = t * 4 + u
                value = features(pos8[b])
                feat8[b] = value
                put_own(b, value)
                put_far(b, value, one_row(which, b))
            return carry

        lax.fori_loop(0, blocks // 4, some, 0)

    def halo_features(turn):
        log_turn = 1 if turn == 2 else 0

        def some(t, carry):
            for side in range(2):
                for u in range(2):
                    i = t * 2 + u
                    got = halo[turn, side, i]
                    value = features(jnp.concatenate([got, got], axis=0))
                    put_far(blocks + side * RIM + i, value, halo[log_turn, side, i][3:4])
                    if turn == 2:
                        put_flags(blocks + side * RIM + i, got[3:4])
            return carry

        lax.fori_loop(0, RIM // 2, some, 0)

    def put_flags(spot, flags):
        flagged[spot] = jnp.where(
            lax.broadcasted_iota(jnp.int32, (16, 128), 0) == 0, flags, F32(1.0)
        ).astype(BF16)

    def sums(columns, picks, b):
        ahead = jnp.concatenate([far[n] for n in picks], axis=1)
        values = jnp.exp(dot_left(ahead, own[b]))
        weights = jnp.concatenate([columns(n) for n in picks], axis=1)
        high = values.astype(BF16)
        low = (values - high.astype(F32)).astype(BF16)
        return dot(weights, high) + dot(weights, low)

    def force_columns(n):
        return far[n, :32, :]

    def force_sums(picks, b):
        found = sums(force_columns, picks, b)
        return found[0:8] + found[8:16] + found[16:24]

    def self_pass(amount, one):
        def some(t, carry):
            found = [one([t * amount + u], t * amount + u) for u in range(amount)]
            for u in range(amount):
                acc[t * amount + u] = found[u]
            return carry

        lax.fori_loop(0, blocks // amount, some, 0)

    def move(b, found):
        value = feat8[b]
        found = found * pltpu.roll(value, 4, 0)
        found = found - pltpu.roll(found, 4, 0)
        vel = vel8[b] + slope * one_row(3, b) * found
        pos = pos8[b] + F32(STEP) * vel
        return pos, vel

    def picks_of(b):
        return [pick[b * NB + k] for k in range(1, NB)]

    def force_pass(turn):
        def rim(t, carry):
            spots = [t * 4 + u for u in range(4)] + [blocks - RIM + t * 4 + u for u in range(4)]
            found = [force_sums(picks_of(b), b) for b in spots]
            for u, b in enumerate(spots):
                pos, vel = move(b, found[u] + acc[b])
                keep(turn, b, pos, vel)
                put_stage(turn + 1, u // 4, t * 4 + u % 4, pos, one_row(1 + turn, b))
            return carry

        lax.fori_loop(0, RIM // 4, rim, 0)
        send_halo(turn + 1)

        def inner(t, carry):
            spots = [RIM + t * 8 + u for u in range(8)]
            found = [force_sums(picks_of(b), b) for b in spots]
            for u, b in enumerate(spots):
                pos, vel = move(b, found[u] + acc[b])
                keep(turn, b, pos, vel)
            return carry

        lax.fori_loop(0, (blocks - 2 * RIM) // 8, inner, 0)

    def keep(turn, b, pos, vel):
        pos8[b] = pos
        if turn == 0:
            vel8[b] = vel
        else:
            state[pl.ds(b, 3, stride=blocks), :] = pos[:3]
            state[pl.ds(3 * blocks + b, 3, stride=blocks), :] = vel[:3]

    def state_copy(side):
        return pltpu.make_async_remote_copy(
            src_ref=state,
            dst_ref=swapped.at[side],
            send_sem=state_send.at[side],
            recv_sem=state_recv.at[side],
            device_id=above if side == 0 else below,
            device_id_type=MESH,
        )

    def finish_halo(turn):
        for side in range(2):
            halo_copy(turn, side).wait()

    for turn in range(2):
        own_features(0)
        self_pass(8, force_sums)
        finish_halo(turn)
        halo_features(turn)
        force_pass(turn)

    state_copy(0).start()
    state_copy(1).start()

    own_features(1)

    def own_flags(b, carry):
        put_flags(b, one_row(2, b))
        return carry

    lax.fori_loop(0, blocks, own_flags, 0)
    flagged[wide] = jnp.zeros((16, 128), BF16)

    def energy_columns(n):
        return flagged[n]

    def energy_sums(picks, b):
        return sums(energy_columns, picks, b)[:8]

    self_pass(8, energy_sums)
    finish_halo(2)
    halo_features(2)

    def energies(t, carry):
        spots = [t * 8 + u for u in range(8)]
        found = [energy_sums(picks_of(b), b) for b in spots]
        inside_sum, mixed_sum = carry
        for u, b in enumerate(spots):
            both = found[u] + acc[b]
            inside = both[0:1]
            every = both[1:2]
            flags = one_row(2, b)
            plain = strength[pl.ds(b, 1), :]
            inside_sum = inside_sum + plain * flags * inside
            mixed_sum = mixed_sum + plain * (
                flags * (every - inside) + (F32(1.0) - flags) * inside
            )
        return inside_sum, mixed_sum

    blank = jnp.zeros((1, 128), F32)
    inside_sum, mixed_sum = lax.fori_loop(0, blocks // 8, energies, (blank, blank))
    mine = jnp.where(row == 0, inside_sum, jnp.where(row == 1, mixed_sum, F32(0.0)))
    energy[here] = mine

    def energy_copy(other, slot):
        return pltpu.make_async_remote_copy(
            src_ref=energy.at[here],
            dst_ref=energy.at[slot],
            send_sem=energy_send.at[other],
            recv_sem=energy_recv.at[slot],
            device_id={"slab": lax.rem(here + other, n_slab)},
            device_id_type=MESH,
        )

    for other in range(1, n_slab):
        energy_copy(other, here).start()

    mate = partner[0]
    taken = accept[0] == 1
    from_below = jnp.full((8, 128), jnp.where(taken & (mate == rep - 1), 1, 0)) == 1
    from_above = jnp.full((8, 128), jnp.where(taken & (mate == rep + 1), 1, 0)) == 1
    for side in range(2):
        state_copy(side).wait()
    for kind, result in ((0, new_pos), (1, new_vel)):

        def choose(t, carry):
            at = pl.ds(pl.multiple_of(t * 8, 8), 8)
            held = pl.ds(pl.multiple_of(3 * kind * blocks + t * 8, 8), 8)
            value = jnp.where(from_below, swapped[0, held, :], state[held, :])
            result[at, :] = jnp.where(from_above, swapped[1, held, :], value)
            return carry

        lax.fori_loop(0, 3 * blocks // 8, choose, 0)

    for other in range(1, n_slab):
        energy_copy(other, lax.rem(here + other, n_slab)).wait_recv()
    every = energy[0]
    for slot in range(1, n_slab):
        every = every + energy[slot]
    every = 0.5 * jnp.sum(every, axis=1, keepdims=True)
    every = jnp.where(row == 2, level, jnp.broadcast_to(every, (8, 128)))
    summary[2] = every

    def summary_copy(side):
        return pltpu.make_async_remote_copy(
            src_ref=summary.at[2],
            dst_ref=summary.at[side],
            send_sem=summary_send.at[side],
            recv_sem=summary_recv.at[side],
            device_id=above if side == 0 else below,
            device_id_type=MESH,
        )

    summary_copy(0).start()
    summary_copy(1).start()
    for other in range(1, n_slab):
        energy_copy(other, here).wait_send()
    summary_copy(0).wait()
    summary_copy(1).wait()
    is_below = jnp.full((8, 128), jnp.where(mate == rep - 1, 1, 0)) == 1
    is_above = jnp.full((8, 128), jnp.where(mate == rep + 1, 1, 0)) == 1
    theirs = jnp.where(is_below, summary[0], jnp.where(is_above, summary[1], every))
    gap = every - theirs
    far_level = theirs[2:3]
    near_level = every[2:3]
    answer = (far_level - near_level) * gap[0:1] + (
        jnp.sqrt(far_level) - jnp.sqrt(near_level)
    ) * gap[1:2]
    answer = answer / F32(total * 128)
    exponent[0] = answer[0, 0]


def shards(
    positions, velocities, strength, inv_mass, solute, scales, neighbours, counts, partner, accept
):
    n_rep = lax.axis_size("rep")
    n_slab = lax.axis_size("slab")
    atoms = positions.shape[2]
    blocks = atoms // 128
    wide = blocks + 2 * RIM
    pairs = 3 * blocks * NB * 128 * 128
    smem = pl.BlockSpec(memory_space=pltpu.SMEM)
    vmem = pl.BlockSpec(memory_space=pltpu.VMEM)
    rowed = (blocks, 128)
    new_pos, new_vel, exponent = pl.pallas_call(
        functools.partial(kernel, n_rep, n_slab, blocks),
        out_shape=(
            jax.ShapeDtypeStruct((3 * blocks, 128), F32),
            jax.ShapeDtypeStruct((3 * blocks, 128), F32),
            jax.ShapeDtypeStruct((1,), F32),
        ),
        in_specs=[smem] * 5 + [vmem] * 5,
        out_specs=(vmem, vmem, smem),
        scratch_shapes=[
            pltpu.SMEM((blocks * NB,), jnp.int32),
            pltpu.VMEM((blocks, 8, 128), F32),
            pltpu.VMEM((blocks, 8, 128), F32),
            pltpu.VMEM((blocks, 8, 128), F32),
            pltpu.VMEM((blocks, 48, 128), BF16),
            pltpu.VMEM((wide + 1, 48, 128), BF16),
            pltpu.VMEM((wide + 1, 16, 128), BF16),
            pltpu.VMEM((blocks, 8, 128), F32),
            pltpu.VMEM((4, blocks, 128), F32),
            pltpu.VMEM((3, 2, RIM, 4, 128), F32),
            pltpu.VMEM((3, 2, RIM, 4, 128), F32),
            pltpu.VMEM((6 * blocks, 128), F32),
            pltpu.VMEM((2, 6 * blocks, 128), F32),
            pltpu.VMEM((n_slab, 8, 128), F32),
            pltpu.VMEM((3, 8, 128), F32),
            pltpu.SemaphoreType.DMA((3, 2)),
            pltpu.SemaphoreType.DMA((3, 2)),
            pltpu.SemaphoreType.DMA((2,)),
            pltpu.SemaphoreType.DMA((2,)),
            pltpu.SemaphoreType.DMA((n_slab,)),
            pltpu.SemaphoreType.DMA((n_slab,)),
            pltpu.SemaphoreType.DMA((2,)),
            pltpu.SemaphoreType.DMA((2,)),
        ],
        compiler_params=pltpu.CompilerParams(
            collective_id=0, has_side_effects=True, vmem_limit_bytes=32 << 20
        ),
        cost_estimate=pl.CostEstimate(
            flops=pairs * 100, bytes_accessed=1 << 20, transcendentals=pairs
        ),
    )(
        scales,
        neighbours.T,
        counts,
        partner,
        accept,
        positions.reshape(3 * blocks, 128),
        velocities.reshape(3 * blocks, 128),
        strength.reshape(rowed),
        inv_mass.reshape(rowed),
        solute.reshape(rowed),
    )
    shape = positions.shape
    return (new_pos.reshape(shape), new_vel.reshape(shape), exponent)


def solution(mesh):
    placed = (
        P("rep", None, "slab"),
        P("rep", None, "slab"),
        P("slab"),
        P("slab"),
        P("slab"),
        P("rep"),
        P("slab", None),
        P("slab"),
        P("rep"),
        P("rep"),
    )
    return jax.shard_map(
        shards,
        mesh=mesh,
        in_specs=placed,
        out_specs=(P("rep", None, "slab"), P("rep", None, "slab"), P("rep")),
        check_vma=False,
    )
```

time: 342 us -> 86 us (0.25)
  matrix products: 196 us -> 0 us
  Pallas kernels: 0 us -> 74.4 us
  starting transfers between devices: 39.8 us -> 0 us
  blocking collectives: 37.2 us -> 0 us
  local copies, waits for them, and re-layouts: 26.5 us -> 5.91 us
  other arithmetic: 20.1 us -> 0 us
  waiting for transfers between devices: 8.43 us -> 0 us
  between operations: 9.63 us -> 4.29 us
    dot_general x36 -> x0, matrix products: 196 us -> none  [the longest x12 67.2 us: field_sums(): jnp.einsum('cbi,cbj->bij', own_c, far_c, precision=HIGH)]
    pallas_call x0 -> x1, Pallas kernels: none -> 74.4 us  [shards(): pl.pallas_call(functools.partial(kernel, n_rep, n_slab, blocks), out_shap...]
    ppermute x14 -> x0, starting transfers between devices: 39.8 us -> none  [the longest x6 26.4 us: shifted(): return lax.ppermute(block, axis, route)]
    psum x1 -> x0, blocking collectives: 37.2 us -> none  [shards(): solute_sum, mixed_sum = lax.psum((solute_part, mixed_part), 'slab')]
    gather x36 -> x0, local copies, waits for them, and re-layouts: 22.5 us -> none  [the longest x12 7.57 us: field_sums(): far_c = jnp.take(blk_c, pick, axis=1)]
    ppermute x14 -> x0, waiting for transfers between devices: 8.43 us -> none  [the longest x4 7.51 us: padded(): lax.ppermute(lax.slice_in_dim(block, block.shape[dim] - width, None, axis...]
    mul x7 -> x0, other arithmetic: 8.29 us -> none  [the longest x2 6.46 us: shards(): far_scale * force_sa_all]
    unnamed x15 -> x16, local copies, waits for them, and re-layouts: 0.97 us -> 5.91 us
  transfers between devices with their start and end apart: 14 -> 0, of which waited for: 3 -> 0; matrix products, arithmetic and copies ran while one was open for 25% -> 0% of each run, Pallas kernels for 0% -> 0%
where the time goes in v1:
time: 86 us; the launch traced here: 84.6 us
  Pallas kernels  74.4 us (87%)
  local copies, waits for them, and re-layouts  5.91 us (7%)
  between operations  4.29 us (5%)
    pallas_call x1, Pallas kernels, shards(): pl.pallas_call(functools.partial(kernel, n_rep, n_slab, blocks), out_shap...  74.4 us
    unnamed x16, local copies, waits for them, and re-layouts  5.91 us

profile of v1, /device:TPU:8, one launch (start us, length us, event | category | flops | bytes accessed | tf_op | source)
XLA Modules:
  0.0 84.6 jit_solution(15700437602321128942)
XLA Ops:
  2.6 0.0 copy-start.5
  2.6 0.0 copy-start.6
  2.6 0.7 copy-done.5
  3.3 0.0 copy-done.6
  3.3 0.0 copy-start
  3.3 0.9 %copy-done = f32[1,3,6144]{2,0,1:T(1,128)S(1)} copy-done((f32[1,3,6144]{2,0,1:T(1,128)S(1)}, f32[1,3,6144]{2,0,1:T(1,128)}, u32[]{:S(2)}) %copy-start) | copy-done | bytes 73752
  4.1 0.0 copy-start.1
  4.1 0.9 %copy-done.1 = f32[1,3,6144]{2,0,1:T(1,128)S(1)} copy-done((f32[1,3,6144]{2,0,1:T(1,128)S(1)}, f32[1,3,6144]{2,0,1:T(1,128)}, u32[]{:S(2)}) %copy-start.1) | copy-done | bytes 73752
  5.0 0.0 copy-start.2
  5.0 0.7 copy-done.2
  5.8 0.0 copy-start.3
  5.8 0.7 copy-done.3
  6.5 0.0 copy-start.4
  6.5 0.7 copy-done.4
  7.2 74.4 %shard_map.121 = (f32[144,128]{1,0:T(8,128)S(1)}, f32[144,128]{1,0:T(8,128)S(1)}, f32[1]{0:T(128)}) custom-call(f32[1]{0:T(128)S(6)} %copy.20.scales, s32[4,48]{1,0:T(4,128)S(1)} %bitcast.15, s32[48]{0:T(128)S(1)} %copy-done.6, s32[1]{0:T(128)S(6)} %copy.21.partner, s32[1]{0:T(128)S(6)} %copy.22.accept, f32[144,128]{1,0:T(8,128)S(1)} %bitcast.10, ...), custom_call_target="tpu_custom_call" | custom-call | flops 943718400 | bytes 1048576 | tf_op jit(solution)/shard_map/pallas_call | solution.py:463
  81.6 0.6 copy.23
  82.3 0.6 copy.24
Async XLA Ops:
  2.6 0.7 copy-start.5
  2.6 0.7 copy-start.6
  3.3 0.9 %copy-start = (f32[1,3,6144]{2,0,1:T(1,128)S(1)}, f32[1,3,6144]{2,0,1:T(1,128)}, u32[]{:S(2)}) copy-start(f32[1,3,6144]{2,0,1:T(1,128)} %param.10) | copy-start | bytes 221188
  4.1 0.9 %copy-start.1 = (f32[1,3,6144]{2,0,1:T(1,128)S(1)}, f32[1,3,6144]{2,0,1:T(1,128)}, u32[]{:S(2)}) copy-start(f32[1,3,6144]{2,0,1:T(1,128)} %param.11) | copy-start | bytes 221188
  5.0 0.7 copy-start.2
  5.8 0.7 copy-start.3
  6.5 0.7 copy-start.4

commit v2 on v1

--- a/solution.py
+++ b/solution.py
@@ -47,6 +47,19 @@
     n_rep,
     n_slab,
     blocks,
+    scales_far,
+    listed_far,
+    counts_far,
+    partner_far,
+    accept_far,
+    positions_far,
+    velocities_far,
+    strength_far,
+    inv_mass_far,
+    solute_far,
+    new_pos,
+    new_vel,
+    exponent,
     scales,
     listed,
     counts,
@@ -57,9 +70,7 @@
     strength,
     inv_mass,
     solute,
-    new_pos,
-    new_vel,
-    exponent,
+    fetch,
     pick,
     pos8,
     vel8,
@@ -92,6 +103,25 @@
     before = {"slab": lax.rem(here + n_slab - 1, n_slab)}
     wide = blocks + 2 * RIM
 
+    fetches = [
+        pltpu.make_async_copy(source, target, fetch.at[i])
+        for i, (source, target) in enumerate(
+            (
+                (strength_far, strength),
+                (solute_far, solute),
+                (inv_mass_far, inv_mass),
+                (scales_far, scales),
+                (positions_far, positions),
+                (velocities_far, velocities),
+                (listed_far, listed),
+                (counts_far, counts),
+                (partner_far, partner),
+                (accept_far, accept),
+            )
+        )
+    ]
+    for copy in fetches:
+        copy.start()
     barrier = pltpu.get_barrier_semaphore()
     for other in range(1, n_slab):
         pl.semaphore_signal(
@@ -108,13 +138,10 @@
     inverse = jnp.where(long, F32(1.0 / periods[0]), F32(1.0 / periods[1]))
     phase = jnp.where(row >= 4, F32(0.25), F32(0.0))
     heights = [p * p / (2.0 * math.pi**2) / (2.0 * SIGMA**2) for p in periods]
-    height = jnp.where(long, F32(heights[0]), F32(heights[1]))
+    height = jnp.where(long, F32(math.sqrt(heights[0])), F32(math.sqrt(heights[1])))
     shift = heights[0] + 2.0 * heights[1]
-    slope = jnp.where(
-        long,
-        F32(STEP * periods[0] / math.pi / (2.0 * SIGMA**2)),
-        F32(STEP * periods[1] / math.pi / (2.0 * SIGMA**2)),
-    )
+    slope = [STEP * p / math.pi / (2.0 * SIGMA**2) / h for p, h in zip(periods, heights)]
+    slope = jnp.where(long, F32(slope[0]), F32(slope[1]))
     slope = jnp.where(is3 | is7, F32(0.0), jnp.where(row >= 4, -slope, slope))
 
     def features(x):
@@ -125,17 +152,20 @@
         value = F32(SINE[-1])
         for c in SINE[-2::-1]:
             value = value * z + F32(c)
-        return value * w
-
-    def put_far(spot, value, log_weight):
+        return value * (w * height)
+
+    fixed = parts(jnp.where(is3, F32(-shift), F32(1.0)))
+
+    def put(spot, value, log_weight, owned):
         value = jnp.where(is3, F32(1.0), jnp.where(is7, log_weight, value))
         a, b, c = parts(value)
         far[spot] = jnp.concatenate([a, b, c, a, b, a], axis=0).astype(BF16)
-
-    def put_own(b, value):
-        value = jnp.where(is3, F32(-shift), jnp.where(is7, F32(1.0), value * height))
-        x, y, z = parts(value)
-        own[b] = jnp.concatenate([x, x, x, y, y, z], axis=0).astype(BF16)
+        if owned:
+            x, y, z = [jnp.where(is3 | is7, k, v) for k, v in zip(fixed, (a, b, c))]
+            own[spot] = jnp.concatenate([x, x, x, y, y, z], axis=0).astype(BF16)
+
+    for copy in fetches:
+        copy.wait()
 
     level = jnp.full((8, 128), scales[0], F32)
     root = jnp.sqrt(level)
@@ -219,55 +249,61 @@
 
     def own_features(which):
         def some(t, carry):
-            for u in range(4):
-                b = t * 4 + u
+            for u in range(12):
+                b = t * 12 + u
                 value = features(pos8[b])
                 feat8[b] = value
-                put_own(b, value)
-                put_far(b, value, one_row(which, b))
+                put(b, value, one_row(which, b), True)
             return carry
 
-        lax.fori_loop(0, blocks // 4, some, 0)
+        lax.fori_loop(0, blocks // 12, some, 0)
 
     def halo_features(turn):
         log_turn = 1 if turn == 2 else 0
 
         def some(t, carry):
             for side in range(2):
-                for u in range(2):
-                    i = t * 2 + u
+                for u in range(4):
+                    i = t * 4 + u
                     got = halo[turn, side, i]
                     value = features(jnp.concatenate([got, got], axis=0))
-                    put_far(blocks + side * RIM + i, value, halo[log_turn, side, i][3:4])
+                    put(blocks + side * RIM + i, value, halo[log_turn, side, i][3:4], False)
                     if turn == 2:
                         put_flags(blocks + side * RIM + i, got[3:4])
             return carry
 
-        lax.fori_loop(0, RIM // 2, some, 0)
+        lax.fori_loop(0, RIM // 4, some, 0)
 
     def put_flags(spot, flags):
         flagged[spot] = jnp.where(
             lax.broadcasted_iota(jnp.int32, (16, 128), 0) == 0, flags, F32(1.0)
         ).astype(BF16)
 
-    def sums(columns, picks, b):
+    def exponents(picks, b):
         ahead = jnp.concatenate([far[n] for n in picks], axis=1)
-        values = jnp.exp(dot_left(ahead, own[b]))
+        return dot_left(ahead, own[b])
+
+    def sums(columns, picks, b, exps):
+        values = jnp.exp(exps)
         weights = jnp.concatenate([columns(n) for n in picks], axis=1)
         high = values.astype(BF16)
         low = (values - high.astype(F32)).astype(BF16)
         return dot(weights, high) + dot(weights, low)
 
+    def all_sums(one, picked):
+        exps = [exponents(picks, b) for picks, b in picked]
+        return [one(picks, b, y) for (picks, b), y in zip(picked, exps)]
+
     def force_columns(n):
         return far[n, :32, :]
 
-    def force_sums(picks, b):
-        found = sums(force_columns, picks, b)
+    def force_sums(picks, b, exps):
+        found = sums(force_columns, picks, b, exps)
         return found[0:8] + found[8:16] + found[16:24]
 
     def self_pass(amount, one):
         def some(t, carry):
-            found = [one([t * amount + u], t * amount + u) for u in range(amount)]
+            found = all_sums(one, [([t * amount + u], t * amount + u) for u in range(amount)])
             for u in range(amount):
                 acc[t * amount + u] = found[u]
             return carry
@@ -287,26 +323,26 @@
 
     def force_pass(turn):
         def rim(t, carry):
-            spots = [t * 4 + u for u in range(4)] + [blocks - RIM + t * 4 + u for u in range(4)]
-            found = [force_sums(picks_of(b), b) for b in spots]
+            spots = [t * 8 + u for u in range(8)] + [blocks - RIM + t * 8 + u for u in range(8)]
+            found = all_sums(force_sums, [(picks_of(b), b) for b in spots])
             for u, b in enumerate(spots):
                 pos, vel = move(b, found[u] + acc[b])
                 keep(turn, b, pos, vel)
-                put_stage(turn + 1, u // 4, t * 4 + u % 4, pos, one_row(1 + turn, b))
+                put_stage(turn + 1, u // 8, t * 8 + u % 8, pos, one_row(1 + turn, b))
             return carry
 
-        lax.fori_loop(0, RIM // 4, rim, 0)
+        lax.fori_loop(0, RIM // 8, rim, 0)
         send_halo(turn + 1)
 
         def inner(t, carry):
-            spots = [RIM + t * 8 + u for u in range(8)]
-            found = [force_sums(picks_of(b), b) for b in spots]
+            spots = [RIM + t * 16 + u for u in range(16)]
+            found = all_sums(force_sums, [(picks_of(b), b) for b in spots])
             for u, b in enumerate(spots):
                 pos, vel = move(b, found[u] + acc[b])
                 keep(turn, b, pos, vel)
             return carry
 
-        lax.fori_loop(0, (blocks - 2 * RIM) // 8, inner, 0)
+        lax.fori_loop(0, (blocks - 2 * RIM) // 16, inner, 0)
 
     def keep(turn, b, pos, vel):
         pos8[b] = pos
@@ -332,7 +368,7 @@
 
     for turn in range(2):
         own_features(0)
-        self_pass(8, force_sums)
+        self_pass(24, force_sums)
         finish_halo(turn)
         halo_features(turn)
         force_pass(turn)
@@ -352,16 +388,16 @@
     def energy_columns(n):
         return flagged[n]
 
-    def energy_sums(picks, b):
-        return sums(energy_columns, picks, b)[:8]
-
-    self_pass(8, energy_sums)
+    def energy_sums(picks, b, exps):
+        return sums(energy_columns, picks, b, exps)[:8]
+
+    self_pass(24, energy_sums)
     finish_halo(2)
     halo_features(2)
 
     def energies(t, carry):
-        spots = [t * 8 + u for u in range(8)]
-        found = [energy_sums(picks_of(b), b) for b in spots]
+        spots = [t * 16 + u for u in range(16)]
+        found = all_sums(energy_sums, [(picks_of(b), b) for b in spots])
         inside_sum, mixed_sum = carry
         for u, b in enumerate(spots):
             both = found[u] + acc[b]
@@ -376,7 +412,7 @@
         return inside_sum, mixed_sum
 
     blank = jnp.zeros((1, 128), F32)
-    inside_sum, mixed_sum = lax.fori_loop(0, blocks // 8, energies, (blank, blank))
+    inside_sum, mixed_sum = lax.fori_loop(0, blocks // 16, energies, (blank, blank))
     mine = jnp.where(row == 0, inside_sum, jnp.where(row == 1, mixed_sum, F32(0.0)))
     energy[here] = mine
 
@@ -467,9 +503,20 @@
             jax.ShapeDtypeStruct((3 * blocks, 128), F32),
             jax.ShapeDtypeStruct((1,), F32),
         ),
-        in_specs=[smem] * 5 + [vmem] * 5,
+        in_specs=[pl.BlockSpec(memory_space=pltpu.HBM)] * 10,
         out_specs=(vmem, vmem, smem),
         scratch_shapes=[
+            pltpu.SMEM((1,), F32),
+            pltpu.SMEM((NB, blocks), jnp.int32),
+            pltpu.SMEM((blocks,), jnp.int32),
+            pltpu.SMEM((1,), jnp.int32),
+            pltpu.SMEM((1,), jnp.int32),
+            pltpu.VMEM((3 * blocks, 128), F32),
+            pltpu.VMEM((3 * blocks, 128), F32),
+            pltpu.VMEM(rowed, F32),
+            pltpu.VMEM(rowed, F32),
+            pltpu.VMEM(rowed, jnp.int32),
+            pltpu.SemaphoreType.DMA((10,)),
             pltpu.SMEM((blocks * NB,), jnp.int32),
             pltpu.VMEM((blocks, 8, 128), F32),
             pltpu.VMEM((blocks, 8, 128), F32),
@@ -495,7 +542,7 @@
             pltpu.SemaphoreType.DMA((2,)),
         ],
         compiler_params=pltpu.CompilerParams(
-            collective_id=0, has_side_effects=True, vmem_limit_bytes=32 << 20
+            collective_id=0, has_side_effects=True, vmem_limit_bytes=56 << 20
         ),
         cost_estimate=pl.CostEstimate(
             flops=pairs * 100, bytes_accessed=1 << 20, transcendentals=pairs

time: 86 us -> 48.3 us (0.56)
  Pallas kernels: 74.4 us -> 41.1 us
  local copies, waits for them, and re-layouts: 5.91 us -> 2.19 us
    pallas_call x1, Pallas kernels: 74.4 us -> 41.1 us  [shards(): pl.pallas_call(functools.partial(kernel, n_rep, n_slab, blocks), out_shap...]
    unnamed x16 -> x4, local copies, waits for them, and re-layouts: 5.91 us -> 2.19 us
where the time goes in v2:
time: 48.3 us; the launch traced here: 47.6 us
  Pallas kernels  41.1 us (85%)
  between operations  4.34 us (9%)
  local copies, waits for them, and re-layouts  2.19 us (5%)
    pallas_call x1, Pallas kernels, shards(): pl.pallas_call(functools.partial(kernel, n_rep, n_slab, blocks), out_shap...  41.1 us
    unnamed x4, local copies, waits for them, and re-layouts  2.19 us

profile of v2, /device:TPU:8, one launch (start us, length us, event | category | flops | bytes accessed | tf_op | source)
XLA Modules:
  0.0 47.6 jit_solution(3518153648761573654)
XLA Ops:
  2.6 41.1 %shard_map.121 = (f32[144,128]{1,0:T(8,128)}, f32[144,128]{1,0:T(8,128)}, f32[1]{0:T(128)}) custom-call(f32[1]{0:T(128)S(6)} %copy.20.scales_far, s32[4,48]{1,0:T(4,128)} %bitcast.15, s32[48]{0:T(128)} %counts_far.1, s32[1]{0:T(128)S(6)} %copy.21.partner_far, s32[1]{0:T(128)S(6)} %copy.22.accept_far, f32[144,128]{1,0:T(8,128)} %bitcast.10, ...), custom_call_target="tpu_custom_call" | custom-call | flops 943718400 | bytes 1048576 | tf_op jit(solution)/shard_map/pallas_call | solution.py:499
  43.7 0.0 copy-start
  43.7 1.6 %copy.23 = f32[1,3,6144]{2,0,1:T(1,128)} copy(f32[1,3,6144]{2,0,1:T(1,128)} %bitcast.9) | data formatting | bytes 147456
  45.3 0.0 copy-done
  45.3 0.6 %copy.24 = f32[1,3,6144]{2,0,1:T(1,128)} copy(f32[1,3,6144]{2,0,1:T(1,128)S(1)} %bitcast.8) | data formatting | bytes 147456
Async XLA Ops:
  43.7 1.6 %copy-start = (f32[144,128]{1,0:T(8,128)S(1)}, f32[144,128]{1,0:T(8,128)}, u32[]{:S(2)}) copy-start(f32[144,128]{1,0:T(8,128)} %get-tuple-element.7) | copy-start | bytes 221188

commit v3 on v2

--- a/solution.py
+++ b/solution.py
@@ -97,8 +97,8 @@
 ):
     rep = lax.axis_index("rep")
     here = lax.axis_index("slab")
-    above = {"rep": lax.rem(rep + 1, n_rep)}
-    below = {"rep": lax.rem(rep + n_rep - 1, n_rep)}
+    above = {"rep": jnp.minimum(rep + 1, n_rep - 1)}
+    below = {"rep": jnp.maximum(rep - 1, 0)}
     after = {"slab": lax.rem(here + 1, n_slab)}
     before = {"slab": lax.rem(here + n_slab - 1, n_slab)}
     wide = blocks + 2 * RIM
@@ -127,8 +127,17 @@
         pl.semaphore_signal(
             barrier, 1, device_id={"slab": lax.rem(here + other, n_slab)}, device_id_type=MESH
         )
-    for other in (below, above):
-        pl.semaphore_signal(barrier, 1, device_id=other, device_id_type=MESH)
+    has_below = rep > 0
+    has_above = rep < n_rep - 1
+
+    @pl.when(has_below)
+    def _():
+        pl.semaphore_signal(barrier, 1, device_id=below, device_id_type=MESH)
+
+    @pl.when(has_above)
+    def _():
+        pl.semaphore_signal(barrier, 1, device_id=above, device_id_type=MESH)
+
 
     row = lax.broadcasted_iota(jnp.int32, (8, 128), 0)
     long = (row == 0) | (row == 4)
@@ -211,7 +220,7 @@
         return carry
 
     lax.fori_loop(0, RIM, stage_first, 0)
-    pl.semaphore_wait(barrier, n_slab - 1 + 2)
+    pl.semaphore_wait(barrier, n_slab - 1 + has_below.astype(jnp.int32) + has_above.astype(jnp.int32))
 
     def halo_copy(turn, side):
         return pltpu.make_async_remote_copy(
@@ -373,8 +382,22 @@
         halo_features(turn)
         force_pass(turn)
 
-    state_copy(0).start()
-    state_copy(1).start()
+    def start_pair(copy):
+        pl.when(has_above)(lambda: copy(0).start())
+        pl.when(has_below)(lambda: copy(1).start())
+
+    def wait_pair(copy):
+        @pl.when(has_above)
+        def _():
+            copy(0).wait_send()
+            copy(1).wait_recv()
+
+        @pl.when(has_below)
+        def _():
+            copy(1).wait_send()
+            copy(0).wait_recv()
+
+    start_pair(state_copy)
 
     own_features(1)
 
@@ -433,8 +456,7 @@
     taken = accept[0] == 1
     from_below = jnp.full((8, 128), jnp.where(taken & (mate == rep - 1), 1, 0)) == 1
     from_above = jnp.full((8, 128), jnp.where(taken & (mate == rep + 1), 1, 0)) == 1
-    for side in range(2):
-        state_copy(side).wait()
+    wait_pair(state_copy)
     for kind, result in ((0, new_pos), (1, new_vel)):
 
         def choose(t, carry):
@@ -465,12 +487,10 @@
             device_id_type=MESH,
         )
 
-    summary_copy(0).start()
-    summary_copy(1).start()
+    start_pair(summary_copy)
     for other in range(1, n_slab):
         energy_copy(other, here).wait_send()
-    summary_copy(0).wait()
-    summary_copy(1).wait()
+    wait_pair(summary_copy)
     is_below = jnp.full((8, 128), jnp.where(mate == rep - 1, 1, 0)) == 1
     is_above = jnp.full((8, 128), jnp.where(mate == rep + 1, 1, 0)) == 1
     theirs = jnp.where(is_below, summary[0], jnp.where(is_above, summary[1], every))

time: 48.3 us -> 47.9 us (level)
  no operation moved by 1% of the time
where the time goes in v3:
time: 47.9 us; the launch traced here: 47.6 us
  Pallas kernels  41.1 us (86%)
  between operations  4.34 us (9%)
  local copies, waits for them, and re-layouts  2.19 us (5%)
    pallas_call x1, Pallas kernels, shards(): pl.pallas_call(functools.partial(kernel, n_rep, n_slab, blocks), out_shap...  41.1 us
    unnamed x4, local copies, waits for them, and re-layouts  2.19 us

profile of v3, /device:TPU:8, one launch (start us, length us, event | category | flops | bytes accessed | tf_op | source)
XLA Modules:
  0.0 47.6 jit_solution(15769683533691076574)
XLA Ops:
  2.6 41.1 %shard_map.121 = (f32[144,128]{1,0:T(8,128)}, f32[144,128]{1,0:T(8,128)}, f32[1]{0:T(128)}) custom-call(f32[1]{0:T(128)S(6)} %copy.20.scales_far, s32[4,48]{1,0:T(4,128)} %bitcast.15, s32[48]{0:T(128)} %counts_far.1, s32[1]{0:T(128)S(6)} %copy.21.partner_far, s32[1]{0:T(128)S(6)} %copy.22.accept_far, f32[144,128]{1,0:T(8,128)} %bitcast.10, ...), custom_call_target="tpu_custom_call" | custom-call | flops 943718400 | bytes 1048576 | tf_op jit(solution)/shard_map/pallas_call | solution.py:519
  43.7 0.0 copy-start
  43.7 1.6 %copy.23 = f32[1,3,6144]{2,0,1:T(1,128)} copy(f32[1,3,6144]{2,0,1:T(1,128)} %bitcast.9) | data formatting | bytes 147456
  45.2 0.0 copy-done
  45.2 0.6 %copy.24 = f32[1,3,6144]{2,0,1:T(1,128)} copy(f32[1,3,6144]{2,0,1:T(1,128)S(1)} %bitcast.8) | data formatting | bytes 147456
Async XLA Ops:
  43.7 1.6 %copy-start = (f32[144,128]{1,0:T(8,128)S(1)}, f32[144,128]{1,0:T(8,128)}, u32[]{:S(2)}) copy-start(f32[144,128]{1,0:T(8,128)} %get-tuple-element.7) | copy-start | bytes 221188

commit v4 on v3

--- a/solution.py
+++ b/solution.py
@@ -85,15 +85,12 @@
     state,
     swapped,
     energy,
-    summary,
     halo_send,
     halo_recv,
     state_send,
     state_recv,
     energy_send,
     energy_recv,
-    summary_send,
-    summary_recv,
 ):
     rep = lax.axis_index("rep")
     here = lax.axis_index("slab")
@@ -123,21 +120,21 @@
     for copy in fetches:
         copy.start()
     barrier = pltpu.get_barrier_semaphore()
-    for other in range(1, n_slab):
-        pl.semaphore_signal(
-            barrier, 1, device_id={"slab": lax.rem(here + other, n_slab)}, device_id_type=MESH
-        )
     has_below = rep > 0
     has_above = rep < n_rep - 1
 
-    @pl.when(has_below)
-    def _():
-        pl.semaphore_signal(barrier, 1, device_id=below, device_id_type=MESH)
-
-    @pl.when(has_above)
-    def _():
-        pl.semaphore_signal(barrier, 1, device_id=above, device_id_type=MESH)
-
+    def mate_slab(line, other):
+        return {**line, "slab": lax.rem(here + other, n_slab)}
+
+    def greet(line, start):
+        for other in range(start, n_slab):
+            pl.semaphore_signal(
+                barrier, 1, device_id=mate_slab(line, other), device_id_type=MESH
+            )
+
+    greet({}, 1)
+    pl.when(has_below)(lambda: greet(below, 0))
+    pl.when(has_above)(lambda: greet(above, 0))
 
     row = lax.broadcasted_iota(jnp.int32, (8, 128), 0)
     long = (row == 0) | (row == 4)
@@ -220,7 +217,8 @@
         return carry
 
     lax.fori_loop(0, RIM, stage_first, 0)
-    pl.semaphore_wait(barrier, n_slab - 1 + has_below.astype(jnp.int32) + has_above.astype(jnp.int32))
+    lines = has_below.astype(jnp.int32) + has_above.astype(jnp.int32)
+    pl.semaphore_wait(barrier, n_slab - 1 + n_slab * lines)
 
     def halo_copy(turn, side):
         return pltpu.make_async_remote_copy(
@@ -436,21 +434,35 @@
 
     blank = jnp.zeros((1, 128), F32)
     inside_sum, mixed_sum = lax.fori_loop(0, blocks // 16, energies, (blank, blank))
-    mine = jnp.where(row == 0, inside_sum, jnp.where(row == 1, mixed_sum, F32(0.0)))
-    energy[here] = mine
-
-    def energy_copy(other, slot):
+    mine = jnp.where(row == 0, inside_sum, jnp.where(row == 1, mixed_sum, level))
+    energy[2, here] = mine
+
+    def energy_copy(kind, other, slot):
+        line = above if kind == 0 else below if kind == 1 else {}
         return pltpu.make_async_remote_copy(
-            src_ref=energy.at[here],
-            dst_ref=energy.at[slot],
-            send_sem=energy_send.at[other],
-            recv_sem=energy_recv.at[slot],
-            device_id={"slab": lax.rem(here + other, n_slab)},
+            src_ref=energy.at[2, here],
+            dst_ref=energy.at[kind, slot],
+            send_sem=energy_send.at[kind, other],
+            recv_sem=energy_recv.at[kind, slot],
+            device_id=mate_slab(line, other),
             device_id_type=MESH,
         )
 
-    for other in range(1, n_slab):
-        energy_copy(other, here).start()
+    def send_energy(kind, start):
+        for other in range(start, n_slab):
+            energy_copy(kind, other, here).start()
+
+    def receive_energy(kind, start):
+        for other in range(start, n_slab):
+            energy_copy(kind, other, lax.rem(here + other, n_slab)).wait_recv()
+
+    def sent_energy(kind, start):
+        for other in range(start, n_slab):
+            energy_copy(kind, other, here).wait_send()
+
+    pl.when(has_above)(lambda: send_energy(0, 0))
+    pl.when(has_below)(lambda: send_energy(1, 0))
+    send_energy(2, 1)
 
     mate = partner[0]
     taken = accept[0] == 1
@@ -468,32 +480,24 @@
 
         lax.fori_loop(0, 3 * blocks // 8, choose, 0)
 
-    for other in range(1, n_slab):
-        energy_copy(other, lax.rem(here + other, n_slab)).wait_recv()
-    every = energy[0]
-    for slot in range(1, n_slab):
-        every = every + energy[slot]
-    every = 0.5 * jnp.sum(every, axis=1, keepdims=True)
-    every = jnp.where(row == 2, level, jnp.broadcast_to(every, (8, 128)))
-    summary[2] = every
-
-    def summary_copy(side):
-        return pltpu.make_async_remote_copy(
-            src_ref=summary.at[2],
-            dst_ref=summary.at[side],
-            send_sem=summary_send.at[side],
-            recv_sem=summary_recv.at[side],
-            device_id=above if side == 0 else below,
-            device_id_type=MESH,
-        )
-
-    start_pair(summary_copy)
-    for other in range(1, n_slab):
-        energy_copy(other, here).wait_send()
-    wait_pair(summary_copy)
+    pl.when(has_above)(lambda: sent_energy(0, 0))
+    pl.when(has_below)(lambda: sent_energy(1, 0))
+    sent_energy(2, 1)
+    receive_energy(2, 1)
+    pl.when(has_below)(lambda: receive_energy(0, 0))
+    pl.when(has_above)(lambda: receive_energy(1, 0))
+
+    def whole(kind):
+        every = energy[kind, 0]
+        for slot in range(1, n_slab):
+            every = every + energy[kind, slot]
+        every = 0.5 * jnp.sum(every, axis=1, keepdims=True)
+        return jnp.where(row == 2, energy[kind, 0], jnp.broadcast_to(every, (8, 128)))
+
+    every = whole(2)
     is_below = jnp.full((8, 128), jnp.where(mate == rep - 1, 1, 0)) == 1
     is_above = jnp.full((8, 128), jnp.where(mate == rep + 1, 1, 0)) == 1
-    theirs = jnp.where(is_below, summary[0], jnp.where(is_above, summary[1], every))
+    theirs = jnp.where(is_below, whole(0), jnp.where(is_above, whole(1), every))
     gap = every - theirs
     far_level = theirs[2:3]
     near_level = every[2:3]
@@ -501,7 +505,7 @@
         jnp.sqrt(far_level) - jnp.sqrt(near_level)
     ) * gap[1:2]
     answer = answer / F32(total * 128)
-    exponent[0] = answer[0, 0]
+    exponent[...] = jnp.broadcast_to(answer, (8, 128))
 
 
 def shards(
@@ -521,10 +525,10 @@
         out_shape=(
             jax.ShapeDtypeStruct((3 * blocks, 128), F32),
             jax.ShapeDtypeStruct((3 * blocks, 128), F32),
-            jax.ShapeDtypeStruct((1,), F32),
+            jax.ShapeDtypeStruct((8, 128), F32),
         ),
         in_specs=[pl.BlockSpec(memory_space=pltpu.HBM)] * 10,
-        out_specs=(vmem, vmem, smem),
+        out_specs=(vmem, vmem, vmem),
         scratch_shapes=[
             pltpu.SMEM((1,), F32),
             pltpu.SMEM((NB, blocks), jnp.int32),
@@ -550,16 +554,13 @@
             pltpu.VMEM((3, 2, RIM, 4, 128), F32),
             pltpu.VMEM((6 * blocks, 128), F32),
             pltpu.VMEM((2, 6 * blocks, 128), F32),
-            pltpu.VMEM((n_slab, 8, 128), F32),
-            pltpu.VMEM((3, 8, 128), F32),
+            pltpu.VMEM((3, n_slab, 8, 128), F32),
             pltpu.SemaphoreType.DMA((3, 2)),
             pltpu.SemaphoreType.DMA((3, 2)),
             pltpu.SemaphoreType.DMA((2,)),
             pltpu.SemaphoreType.DMA((2,)),
-            pltpu.SemaphoreType.DMA((n_slab,)),
-            pltpu.SemaphoreType.DMA((n_slab,)),
-            pltpu.SemaphoreType.DMA((2,)),
-            pltpu.SemaphoreType.DMA((2,)),
+            pltpu.SemaphoreType.DMA((3, n_slab)),
+            pltpu.SemaphoreType.DMA((3, n_slab)),
         ],
         compiler_params=pltpu.CompilerParams(
             collective_id=0, has_side_effects=True, vmem_limit_bytes=56 << 20
@@ -580,7 +581,7 @@
         solute.reshape(rowed),
     )
     shape = positions.shape
-    return (new_pos.reshape(shape), new_vel.reshape(shape), exponent)
+    return (new_pos.reshape(shape), new_vel.reshape(shape), exponent[0, :1])
 
 
 def solution(mesh):

time: 47.9 us -> 45.2 us (0.944)
  Pallas kernels: 41.1 us -> 38.8 us
  between operations: 4.34 us -> 2.58 us
  local copies, waits for them, and re-layouts: 2.19 us -> 3.37 us
    pallas_call x1, Pallas kernels: 41.1 us -> 38.8 us  [shards(): pl.pallas_call(functools.partial(kernel, n_rep, n_slab, blocks), out_shap...]
    slice x0 -> x1, local copies, waits for them, and re-layouts: none -> 1.19 us  [shards(): return (new_pos.reshape(shape), new_vel.reshape(shape), exponent[0, :1])]
where the time goes in v4:
time: 45.2 us; the launch traced here: 44.7 us
  Pallas kernels  38.8 us (86%)
  local copies, waits for them, and re-layouts  3.37 us (7%)
  between operations  2.58 us (6%)
    pallas_call x1, Pallas kernels, shards(): pl.pallas_call(functools.partial(kernel, n_rep, n_slab, blocks), out_shap...  38.8 us
    unnamed x4, local copies, waits for them, and re-layouts  2.19 us
    slice x1, local copies, waits for them, and re-layouts, shards(): return (new_pos.reshape(shape), new_vel.reshape(shape), exponent[0, :1])  1.19 us

profile of v4, /device:TPU:8, one launch (start us, length us, event | category | flops | bytes accessed | tf_op | source)
XLA Modules:
  0.0 44.7 jit_solution(7813808880977952250)
XLA Ops:
  2.6 38.8 %shard_map.121 = (f32[144,128]{1,0:T(8,128)}, f32[144,128]{1,0:T(8,128)}, f32[8,128]{1,0:T(8,128)}) custom-call(f32[1]{0:T(128)S(6)} %copy.19.scales_far, s32[4,48]{1,0:T(4,128)} %bitcast.16, s32[48]{0:T(128)} %counts_far.1, s32[1]{0:T(128)S(6)} %copy.20.partner_far, s32[1]{0:T(128)S(6)} %copy.21.accept_far, f32[144,128]{1,0:T(8,128)} %bitcast.11, ...), custom_call_target="tpu_custom_call" | custom-call | flops 943718400 | bytes 1048576 | tf_op jit(solution)/shard_map/pallas_call | solution.py:523
  41.3 1.2 %slice.3 = f32[1,1]{1,0:T(1,128)} slice(f32[8,128]{1,0:T(8,128)} %get-tuple-element.8), slice={[0:1], [0:1]} | slice | bytes 8 | tf_op jit(solution)/shard_map/slice | solution.py:584
  42.5 0.0 copy-start
  42.5 1.6 %copy.22 = f32[1,3,6144]{2,0,1:T(1,128)} copy(f32[1,3,6144]{2,0,1:T(1,128)} %bitcast.10) | data formatting | bytes 147456
  44.1 0.0 copy-done
  44.1 0.6 %copy.23 = f32[1,3,6144]{2,0,1:T(1,128)} copy(f32[1,3,6144]{2,0,1:T(1,128)S(1)} %bitcast.9) | data formatting | bytes 147456
Async XLA Ops:
  42.5 1.6 %copy-start = (f32[144,128]{1,0:T(8,128)S(1)}, f32[144,128]{1,0:T(8,128)}, u32[]{:S(2)}) copy-start(f32[144,128]{1,0:T(8,128)} %get-tuple-element.7) | copy-start | bytes 221188

commit v5 on v4

--- a/solution.py
+++ b/solution.py
@@ -508,6 +508,12 @@
     exponent[...] = jnp.broadcast_to(answer, (8, 128))
 
 
+def hand_over(pos, vel, tile, new_pos, new_vel, exponent):
+    new_pos[...] = pos[...]
+    new_vel[...] = vel[...]
+    exponent[...] = tile[0:1, 0:1]
+
+
 def shards(
     positions, velocities, strength, inv_mass, solute, scales, neighbours, counts, partner, accept
 ):
@@ -519,6 +525,7 @@
     pairs = 3 * blocks * NB * 128 * 128
     smem = pl.BlockSpec(memory_space=pltpu.SMEM)
     vmem = pl.BlockSpec(memory_space=pltpu.VMEM)
+    far = pl.BlockSpec(memory_space=pltpu.HBM)
     rowed = (blocks, 128)
     new_pos, new_vel, exponent = pl.pallas_call(
         functools.partial(kernel, n_rep, n_slab, blocks),
@@ -581,7 +588,17 @@
         solute.reshape(rowed),
     )
     shape = positions.shape
-    return (new_pos.reshape(shape), new_vel.reshape(shape), exponent[0, :1])
+    new_pos, new_vel, exponent = pl.pallas_call(
+        hand_over,
+        out_shape=(
+            jax.ShapeDtypeStruct((3 * blocks, 128), F32),
+            jax.ShapeDtypeStruct((3 * blocks, 128), F32),
+            jax.ShapeDtypeStruct((1, 1), F32),
+        ),
+        in_specs=[vmem, vmem, vmem],
+        out_specs=(vmem, vmem, vmem),
+    )(new_pos, new_vel, exponent)
+    return (new_pos.reshape(shape), new_vel.reshape(shape), exponent.reshape(1))
 
 
 def solution(mesh):

time: 45.2 us -> 43.4 us (0.960)
  local copies, waits for them, and re-layouts: 3.37 us -> 0 us
  Pallas kernels: 38.8 us -> 40.3 us
    unnamed x4 -> x0, local copies, waits for them, and re-layouts: 2.19 us -> none
    pallas_call x0 -> x1, Pallas kernels: none -> 1.59 us  [shards(): pl.pallas_call(hand_over, out_shape=(jax.ShapeDtypeStruct((3 * blocks, 12...]
    slice x1 -> x0, local copies, waits for them, and re-layouts: 1.19 us -> none  [shards(): return (new_pos.reshape(shape), new_vel.reshape(shape), exponent[0, :1])]
where the time goes in v5:
time: 43.4 us; the launch traced here: 42.9 us
  Pallas kernels  40.3 us (93%)
  between operations  2.58 us (6%)
    pallas_call x1, Pallas kernels, shards(): pl.pallas_call(functools.partial(kernel, n_rep, n_slab, blocks), out_shap...  38.8 us
    pallas_call x1, Pallas kernels, shards(): pl.pallas_call(hand_over, out_shape=(jax.ShapeDtypeStruct((3 * blocks, 12...  1.59 us

profile of v5, /device:TPU:8, one launch (start us, length us, event | category | flops | bytes accessed | tf_op | source)
XLA Modules:
  0.0 42.9 jit_solution(5687747008733766091)
XLA Ops:
  2.6 38.8 %shard_map.121 = (f32[144,128]{1,0:T(8,128)}, f32[144,128]{1,0:T(8,128)}, f32[8,128]{1,0:T(8,128)}) custom-call(f32[1]{0:T(128)S(6)} %copy.17.scales_far, s32[4,48]{1,0:T(4,128)} %bitcast.16, s32[48]{0:T(128)} %counts_far.1, s32[1]{0:T(128)S(6)} %copy.18.partner_far, s32[1]{0:T(128)S(6)} %copy.19.accept_far, f32[144,128]{1,0:T(8,128)} %bitcast.9, ...), custom_call_target="tpu_custom_call" | custom-call | flops 943718400 | bytes 1048576 | tf_op jit(solution)/shard_map/pallas_call | solution.py:530
  41.3 1.6 %shard_map.122 = (f32[144,128]{1,0:T(8,128)}, f32[144,128]{1,0:T(8,128)}, f32[1,1]{1,0:T(1,128)}) custom-call(f32[144,128]{1,0:T(8,128)} %get-tuple-element.9.pos, f32[144,128]{1,0:T(8,128)} %get-tuple-element.10.vel, f32[8,128]{1,0:T(8,128)} %get-tuple-element.11.tile), custom_call_target="tpu_custom_call" | custom-call | tf_op jit(solution)/shard_map/pallas_call | solution.py:591

commit v6 on v5

--- a/solution.py
+++ b/solution.py
@@ -375,7 +375,7 @@
 
     for turn in range(2):
         own_features(0)
-        self_pass(24, force_sums)
+        self_pass(48, force_sums)
         finish_halo(turn)
         halo_features(turn)
         force_pass(turn)
@@ -412,12 +412,12 @@
     def energy_sums(picks, b, exps):
         return sums(energy_columns, picks, b, exps)[:8]
 
-    self_pass(24, energy_sums)
+    self_pass(48, energy_sums)
     finish_halo(2)
     halo_features(2)
 
     def energies(t, carry):
-        spots = [t * 16 + u for u in range(16)]
+        spots = [t * 24 + u for u in range(24)]
         found = all_sums(energy_sums, [(picks_of(b), b) for b in spots])
         inside_sum, mixed_sum = carry
         for u, b in enumerate(spots):
@@ -433,7 +433,7 @@
         return inside_sum, mixed_sum
 
     blank = jnp.zeros((1, 128), F32)
-    inside_sum, mixed_sum = lax.fori_loop(0, blocks // 16, energies, (blank, blank))
+    inside_sum, mixed_sum = lax.fori_loop(0, blocks // 24, energies, (blank, blank))
     mine = jnp.where(row == 0, inside_sum, jnp.where(row == 1, mixed_sum, level))
     energy[2, here] = mine
 

time: 43.4 us -> 43.2 us (level)
  no operation moved by 1% of the time
where the time goes in v6:
time: 43.2 us; the launch traced here: 42.7 us
  Pallas kernels  40.1 us (93%)
  between operations  2.58 us (6%)
    pallas_call x1, Pallas kernels, shards(): pl.pallas_call(functools.partial(kernel, n_rep, n_slab, blocks), out_shap...  38.5 us
    pallas_call x1, Pallas kernels, shards(): pl.pallas_call(hand_over, out_shape=(jax.ShapeDtypeStruct((3 * blocks, 12...  1.59 us

profile of v6, /device:TPU:8, one launch (start us, length us, event | category | flops | bytes accessed | tf_op | source)
XLA Modules:
  0.0 42.7 jit_solution(13140121927968555444)
XLA Ops:
  2.6 38.5 %shard_map.121 = (f32[144,128]{1,0:T(8,128)}, f32[144,128]{1,0:T(8,128)}, f32[8,128]{1,0:T(8,128)}) custom-call(f32[1]{0:T(128)S(6)} %copy.17.scales_far, s32[4,48]{1,0:T(4,128)} %bitcast.16, s32[48]{0:T(128)} %counts_far.1, s32[1]{0:T(128)S(6)} %copy.18.partner_far, s32[1]{0:T(128)S(6)} %copy.19.accept_far, f32[144,128]{1,0:T(8,128)} %bitcast.9, ...), custom_call_target="tpu_custom_call" | custom-call | flops 943718400 | bytes 1048576 | tf_op jit(solution)/shard_map/pallas_call | solution.py:530
  41.1 1.6 %shard_map.122 = (f32[144,128]{1,0:T(8,128)}, f32[144,128]{1,0:T(8,128)}, f32[1,1]{1,0:T(1,128)}) custom-call(f32[144,128]{1,0:T(8,128)} %get-tuple-element.9.pos, f32[144,128]{1,0:T(8,128)} %get-tuple-element.10.vel, f32[8,128]{1,0:T(8,128)} %get-tuple-element.11.tile), custom_call_target="tpu_custom_call" | custom-call | tf_op jit(solution)/shard_map/pallas_call | solution.py:591

commit v7 on v5

--- a/solution.py
+++ b/solution.py
@@ -57,9 +57,12 @@
     strength_far,
     inv_mass_far,
     solute_far,
+    new_pos_far,
+    new_vel_far,
+    exponent,
     new_pos,
     new_vel,
-    exponent,
+    leave,
     scales,
     listed,
     counts,
@@ -170,24 +173,19 @@
             x, y, z = [jnp.where(is3 | is7, k, v) for k, v in zip(fixed, (a, b, c))]
             own[spot] = jnp.concatenate([x, x, x, y, y, z], axis=0).astype(BF16)
 
-    for copy in fetches:
+    for copy in fetches[:5]:
         copy.wait()
 
     level = jnp.full((8, 128), scales[0], F32)
     root = jnp.sqrt(level)
 
-    def atom_rows(t, carry):
-        at = pl.ds(pl.multiple_of(t * 8, 8), 8)
-        plain = strength[at, :]
-        chosen = solute[at, :] == 1
-        scaled = plain * jnp.where(chosen, root, F32(1.0))
-        rows[0, at, :] = jnp.log(scaled)
-        rows[1, at, :] = jnp.log(plain)
-        rows[2, at, :] = jnp.where(chosen, F32(1.0), F32(0.0))
-        rows[3, at, :] = scaled * inv_mass[at, :]
-        return carry
-
-    lax.fori_loop(0, blocks // 8, atom_rows, 0)
+    plain = strength[...]
+    chosen = solute[...] == 1
+    scaled = plain * jnp.where(chosen, root[0:1], F32(1.0))
+    rows[0] = jnp.log(scaled)
+    rows[1] = jnp.log(plain)
+    rows[2] = jnp.where(chosen, F32(1.0), F32(0.0))
+    rows[3] = scaled * inv_mass[...]
 
     def one_row(which, b):
         return rows[which, pl.ds(b, 1), :]
@@ -195,28 +193,15 @@
     def put_stage(turn, side, i, x, extra):
         stage[turn, side, i] = jnp.where(is3, extra, x)[:4]
 
-    def load(b):
-        blank = jnp.zeros((1, 128), F32)
-        x = positions[pl.ds(b, 3, stride=blocks), :]
-        v = velocities[pl.ds(b, 3, stride=blocks), :]
-        pos8[b] = jnp.concatenate([x, blank, x, blank], axis=0)
-        vel8[b] = jnp.concatenate([v, blank, v, blank], axis=0)
-
-    def load_some(t, carry):
+    def stage_first(t, carry):
         for u in range(4):
-            load(t * 4 + u)
+            i = t * 4 + u
+            for side, b in ((0, i), (1, blocks - RIM + i)):
+                x = positions[pl.ds(b, 3, stride=blocks), :]
+                stage[0, side, i] = jnp.concatenate([x, one_row(0, b)], axis=0)
         return carry
 
-    lax.fori_loop(0, blocks // 4, load_some, 0)
-
-    def stage_first(i, carry):
-        low = i
-        high = blocks - RIM + i
-        put_stage(0, 0, i, pos8[low], one_row(0, low))
-        put_stage(0, 1, i, pos8[high], one_row(0, high))
-        return carry
-
-    lax.fori_loop(0, RIM, stage_first, 0)
+    lax.fori_loop(0, RIM // 4, stage_first, 0)
     lines = has_below.astype(jnp.int32) + has_above.astype(jnp.int32)
     pl.semaphore_wait(barrier, n_slab - 1 + n_slab * lines)
 
@@ -235,6 +220,22 @@
             halo_copy(turn, side).start()
 
     send_halo(0)
+    for copy in fetches[5:]:
+        copy.wait()
+
+    def load(b):
+        blank = jnp.zeros((1, 128), F32)
+        x = positions[pl.ds(b, 3, stride=blocks), :]
+        v = velocities[pl.ds(b, 3, stride=blocks), :]
+        pos8[b] = jnp.concatenate([x, blank, x, blank], axis=0)
+        vel8[b] = jnp.concatenate([v, blank, v, blank], axis=0)
+
+    def load_some(t, carry):
+        for u in range(4):
+            load(t * 4 + u)
+        return carry
+
+    lax.fori_loop(0, blocks // 4, load_some, 0)
 
     first = here * blocks
     total = n_slab * blocks
@@ -480,6 +481,13 @@
 
         lax.fori_loop(0, 3 * blocks // 8, choose, 0)
 
+    leaves = [
+        pltpu.make_async_copy(new_pos, new_pos_far, leave.at[0]),
+        pltpu.make_async_copy(new_vel, new_vel_far, leave.at[1]),
+    ]
+    for copy in leaves:
+        copy.start()
+
     pl.when(has_above)(lambda: sent_energy(0, 0))
     pl.when(has_below)(lambda: sent_energy(1, 0))
     sent_energy(2, 1)
@@ -506,6 +514,8 @@
     ) * gap[1:2]
     answer = answer / F32(total * 128)
     exponent[...] = jnp.broadcast_to(answer, (8, 128))
+    for copy in leaves:
+        copy.wait()
 
 
 def hand_over(pos, vel, tile, new_pos, new_vel, exponent):
@@ -535,8 +545,11 @@
             jax.ShapeDtypeStruct((8, 128), F32),
         ),
         in_specs=[pl.BlockSpec(memory_space=pltpu.HBM)] * 10,
-        out_specs=(vmem, vmem, vmem),
+        out_specs=(far, far, vmem),
         scratch_shapes=[
+            pltpu.VMEM((3 * blocks, 128), F32),
+            pltpu.VMEM((3 * blocks, 128), F32),
+            pltpu.SemaphoreType.DMA((2,)),
             pltpu.SMEM((1,), F32),
             pltpu.SMEM((NB, blocks), jnp.int32),
             pltpu.SMEM((blocks,), jnp.int32),

time: 43.4 us -> 43.4 us (level)
  no operation moved by 1% of the time
where the time goes in v7:
time: 43.4 us; the launch traced here: 42.9 us
  Pallas kernels  40.3 us (93%)
  between operations  2.58 us (6%)
    pallas_call x1, Pallas kernels, shards(): pl.pallas_call(functools.partial(kernel, n_rep, n_slab, blocks), out_shap...  38.8 us
    pallas_call x1, Pallas kernels, shards(): pl.pallas_call(hand_over, out_shape=(jax.ShapeDtypeStruct((3 * blocks, 12...  1.59 us

profile of v7, /device:TPU:8, one launch (start us, length us, event | category | flops | bytes accessed | tf_op | source)
XLA Modules:
  0.0 42.9 jit_solution(15571944120111014578)
XLA Ops:
  2.6 38.8 %shard_map.121 = (f32[144,128]{1,0:T(8,128)}, f32[144,128]{1,0:T(8,128)}, f32[8,128]{1,0:T(8,128)}) custom-call(f32[1]{0:T(128)S(6)} %copy.17.scales_far, s32[4,48]{1,0:T(4,128)} %bitcast.16, s32[48]{0:T(128)} %counts_far.1, s32[1]{0:T(128)S(6)} %copy.18.partner_far, s32[1]{0:T(128)S(6)} %copy.19.accept_far, f32[144,128]{1,0:T(8,128)} %bitcast.9, ...), custom_call_target="tpu_custom_call" | custom-call | flops 943718400 | bytes 1048576 | tf_op jit(solution)/shard_map/pallas_call | solution.py:540
  41.3 1.6 %shard_map.122 = (f32[144,128]{1,0:T(8,128)}, f32[144,128]{1,0:T(8,128)}, f32[1,1]{1,0:T(1,128)}) custom-call(f32[144,128]{1,0:T(8,128)} %get-tuple-element.9.pos, f32[144,128]{1,0:T(8,128)} %get-tuple-element.10.vel, f32[8,128]{1,0:T(8,128)} %get-tuple-element.11.tile), custom_call_target="tpu_custom_call" | custom-call | tf_op jit(solution)/shard_map/pallas_call | solution.py:604

commit v8 on v5

--- a/solution.py
+++ b/solution.py
@@ -132,9 +132,9 @@
                 barrier, 1, device_id=mate_slab(line, other), device_id_type=MESH
             )
 
+    pl.when(has_above)(lambda: greet(above, 0))
     greet({}, 1)
     pl.when(has_below)(lambda: greet(below, 0))
-    pl.when(has_above)(lambda: greet(above, 0))
 
     row = lax.broadcasted_iota(jnp.int32, (8, 128), 0)
     long = (row == 0) | (row == 4)

time: 43.4 us -> 43.3 us (level)
  no operation moved by 1% of the time
where the time goes in v8:
time: 43.3 us; the launch traced here: 42.6 us
  Pallas kernels  40.1 us (93%)
  between operations  2.58 us (6%)
    pallas_call x1, Pallas kernels, shards(): pl.pallas_call(functools.partial(kernel, n_rep, n_slab, blocks), out_shap...  38.5 us
    pallas_call x1, Pallas kernels, shards(): pl.pallas_call(hand_over, out_shape=(jax.ShapeDtypeStruct((3 * blocks, 12...  1.59 us

profile of v8, /device:TPU:8, one launch (start us, length us, event | category | flops | bytes accessed | tf_op | source)
XLA Modules:
  0.0 42.6 jit_solution(17082814636512623152)
XLA Ops:
  2.6 38.5 %shard_map.121 = (f32[144,128]{1,0:T(8,128)}, f32[144,128]{1,0:T(8,128)}, f32[8,128]{1,0:T(8,128)}) custom-call(f32[1]{0:T(128)S(6)} %copy.17.scales_far, s32[4,48]{1,0:T(4,128)} %bitcast.16, s32[48]{0:T(128)} %counts_far.1, s32[1]{0:T(128)S(6)} %copy.18.partner_far, s32[1]{0:T(128)S(6)} %copy.19.accept_far, f32[144,128]{1,0:T(8,128)} %bitcast.9, ...), custom_call_target="tpu_custom_call" | custom-call | flops 943718400 | bytes 1048576 | tf_op jit(solution)/shard_map/pallas_call | solution.py:530
  41.1 1.6 %shard_map.122 = (f32[144,128]{1,0:T(8,128)}, f32[144,128]{1,0:T(8,128)}, f32[1,1]{1,0:T(1,128)}) custom-call(f32[144,128]{1,0:T(8,128)} %get-tuple-element.9.pos, f32[144,128]{1,0:T(8,128)} %get-tuple-element.10.vel, f32[8,128]{1,0:T(8,128)} %get-tuple-element.11.tile), custom_call_target="tpu_custom_call" | custom-call | tf_op jit(solution)/shard_map/pallas_call | solution.py:591
